TPU v7x, 256 devices: a whole 4x4x8 slice. The times are simulated.
256 devices in a mesh: space: 64 (over y_hi, z, x), chan: 4 (over y_lo, core).
Axes of the slice: x: 4, y: 4 (y_hi: 2, y_lo: 2; y = y_hi * 2 + y_lo), z: 8, core: 2. Of those that a mesh axis runs over, the one named last changes fastest.
Arguments:
- grid_state: bfloat16 [192, 720, 512], P('space'), may hold values from -6 to 6
- fold_columns: int32 [720], replicated, may hold values from 0 to 719, each once
- mesh_state: bfloat16 [10240, 512], P('space', 'chan'), may hold values from -6 to 6
- edge_state: bfloat16 [327680, 512], P('space'), may hold values from -6 to 6
- conv_weight: bfloat16 [3, 3, 512, 512], P(None, None, None, 'chan'), may hold values from -0.09375 to 0.09375
- conv_bias: bfloat16 [512], P('chan'), may hold values from -3 to 3
- source_weight: bfloat16 [512, 512], P(None, 'chan'), may hold values from -0.25 to 0.25
- target_weight: bfloat16 [512, 512], P(None, 'chan'), may hold values from -0.25 to 0.25
- edge_weight: bfloat16 [512, 512], P(None, 'chan'), may hold values from -0.25 to 0.25
- edge_bias: bfloat16 [512], P('chan'), may hold values from -3 to 3
- message_weight: bfloat16 [512, 512], replicated, may hold values from -0.25 to 0.25
- self_weight: bfloat16 [512, 512], P(None, 'chan'), may hold values from -0.1875 to 0.1875
- inbox_weight: bfloat16 [512, 512], P(None, 'chan'), may hold values from -0.1875 to 0.1875
- node_bias: bfloat16 [512], P('chan'), may hold values from -3 to 3
- output_weight: bfloat16 [512, 512], replicated
- output_gain: float32 [512], replicated, may hold values from 0.1 to 1.9
- cell_node: int32 [192, 720], P('space'), may hold values from 0 to 159
- cell_weight: float32 [192, 720], P('space'), may hold values from 0.2 to 1
- edge_source: int32 [327680], P('space'), may hold values from 0 to 2207, as said below
- edge_target: int32 [327680], P('space'), may hold values from 0 to 159
- edge_count: int32 [64], P('space'), may hold values from 1024 to 5120, as said below
- send_rows: int32 [64, 64, 32], P('space'), may hold values from 0 to 159
- read_node: int32 [3, 192, 720], P(None, 'space'), may hold values from 0 to 159
- read_weight: float32 [3, 192, 720], P(None, 'space'), may hold values from 0.2 to 1
Outputs:
- node_out: bfloat16 [10240, 512], P('space', 'chan')
- grid_out: bfloat16 [192, 720, 512], P('space', None, 'chan')
Inputs may be any that keep to these rules, and one draw needn't show every extreme that they name: fold_columns is a permutation of the 720 columns. send_rows[q, p, k] is a node of partition q, by its index within q, sent to partition p in slot k. `edge_source`: a value below 160 names a node of the edge's own partition; a larger value names slot (s - 160) % 32 of the rows sent by partition (s - 160) // 32. The live edges of a partition are its first edge_count slots; some partition has 5120 live edges in every draw.
All inputs are finite; a program needn't handle non-finite values.
Results may differ from a plain program's by a relative error of at most 0.0095.
Values may be sent and summed in bfloat16 or wider, within the bound.
A program may use at most 64 MiB of HBM per device.

v0:
```python
import jax
import jax.numpy as jnp
from jax import lax
from jax.sharding import PartitionSpec as P

norm_eps = 1e-05


def with_halo(value, sides, width):
    for axis, dim in sides:
        size, length = (lax.axis_size(axis), value.shape[dim])
        up = [(i, (i + 1) % size) for i in range(size - 1)]
        down = [(j, i) for i, j in up]
        last = lax.slice_in_dim(value, length - width, length, axis=dim)
        leading = lax.slice_in_dim(value, 0, width, axis=dim)
        before = lax.ppermute(last, axis, up)
        after = lax.ppermute(leading, axis, down)
        value = jnp.concatenate([before, value, after], axis=dim)
    return value


def project_rows(partial_rows, full_weight):
    shard_cols = partial_rows.shape[1]
    first_row = lax.axis_index("chan") * shard_cols
    rows_used = lax.dynamic_slice_in_dim(full_weight, first_row, shard_cols, 0)
    partial_sum = jnp.dot(partial_rows, rows_used, preferred_element_type=jnp.float32)
    return lax.psum(partial_sum.astype(jnp.bfloat16), "chan").astype(jnp.float32)


def shards(
    grid_state,
    fold_columns,
    mesh_state,
    edge_state,
    conv_weight,
    conv_bias,
    source_weight,
    target_weight,
    edge_weight,
    edge_bias,
    message_weight,
    self_weight,
    inbox_weight,
    node_bias,
    output_weight,
    output_gain,
    cell_node,
    cell_weight,
    edge_source,
    edge_target,
    edge_count,
    send_rows,
    read_node,
    read_weight,
):
    band_rows, band_cols, features = grid_state.shape
    shard_cols = conv_weight.shape[3]
    chan_start = lax.axis_index("chan") * shard_cols
    node_count = mesh_state.shape[0]
    tall_grid = with_halo(grid_state, (("space", 0),), 1)
    south_rim = tall_grid[0]
    north_rim = tall_grid[-1]
    top_device = lax.axis_index("space") == lax.axis_size("space") - 1
    north_row = jnp.where(top_device, grid_state[-1][fold_columns], north_rim)
    tall_grid = jnp.concatenate([south_rim[None], grid_state, north_row[None]], axis=0)
    padded = jnp.concatenate([tall_grid[:, -1:], tall_grid, tall_grid[:, :1]], axis=1)
    summed = jnp.zeros((band_rows * band_cols, shard_cols), jnp.float32)
    for shift_row in range(3):
        for shift_col in range(3):
            window = padded[
                shift_row : shift_row + band_rows, shift_col : shift_col + band_cols, :
            ].reshape(band_rows * band_cols, features)
            summed = summed + jnp.dot(
                window, conv_weight[shift_row, shift_col], preferred_element_type=jnp.float32
            )
    conv = summed + conv_bias.astype(jnp.float32)
    node_ids = jnp.arange(node_count, dtype=jnp.int32)[:, None]
    cell_match = node_ids == cell_node.reshape(1, -1)
    cell_incidence = jnp.where(cell_match, cell_weight.reshape(1, -1), 0.0)
    agg = jnp.dot(
        cell_incidence,
        jax.nn.silu(conv),
        precision=lax.Precision.HIGHEST,
        preferred_element_type=jnp.float32,
    )
    nodes_part = (mesh_state.astype(jnp.float32) + agg).astype(jnp.bfloat16)
    nodes = lax.all_gather(nodes_part, "chan", axis=1, tiled=True)
    edge_term = jnp.dot(
        edge_state, edge_weight, preferred_element_type=jnp.float32
    ) + edge_bias.astype(jnp.float32)
    sent = jnp.dot(nodes, source_weight, preferred_element_type=jnp.float32).astype(jnp.bfloat16)
    recv = jnp.dot(nodes, target_weight, preferred_element_type=jnp.float32)
    outgoing = sent[send_rows[0]]
    incoming = lax.all_to_all(outgoing, "space", split_axis=0, concat_axis=0, tiled=True)
    source_table = jnp.concatenate([sent, incoming.reshape(-1, shard_cols)], axis=0)
    pre_act = source_table[edge_source].astype(jnp.float32) + recv[edge_target] + edge_term
    edge_slots = edge_state.shape[0]
    live_mask = (jnp.arange(edge_slots, dtype=jnp.int32) < edge_count[0]).astype(jnp.bfloat16)
    edge_hidden = jax.nn.silu(pre_act).astype(jnp.bfloat16) * live_mask[:, None]
    edge_incidence = (node_ids == edge_target.reshape(1, -1)).astype(jnp.bfloat16)
    pooled = jnp.dot(edge_incidence, edge_hidden, preferred_element_type=jnp.float32).astype(
        jnp.bfloat16
    )
    message = project_rows(pooled, message_weight).astype(jnp.bfloat16)
    node_pre = jnp.dot(nodes, self_weight, preferred_element_type=jnp.float32) + jnp.dot(
        message, inbox_weight, preferred_element_type=jnp.float32
    )
    node_hidden = jax.nn.silu(node_pre + node_bias.astype(jnp.float32)).astype(jnp.bfloat16)
    update = project_rows(node_hidden, output_weight)
    row_mean = jnp.mean(update, axis=1, keepdims=True)
    row_var = jnp.mean(jnp.square(update - row_mean), axis=1, keepdims=True)
    normed = output_gain * (update - row_mean) * lax.rsqrt(row_var + norm_eps)
    normed_part = lax.dynamic_slice_in_dim(normed, chan_start, shard_cols, 1)
    node_out = (nodes_part.astype(jnp.float32) + normed_part).astype(jnp.bfloat16)
    grid_part = lax.dynamic_slice_in_dim(grid_state, chan_start, shard_cols, 2)
    grid_sum = grid_part.astype(jnp.float32)
    for corner in range(3):
        grid_sum = grid_sum + read_weight[corner][..., None] * node_out[read_node[corner]].astype(
            jnp.float32
        )
    grid_out = grid_sum.astype(jnp.bfloat16)
    return (node_out, grid_out)


def solution(mesh):
    in_specs = (
        P("space", None, None),
        P(),
        P("space", "chan"),
        P("space", None),
        P(None, None, None, "chan"),
        P("chan"),
        P(None, "chan"),
        P(None, "chan"),
        P(None, "chan"),
        P("chan"),
        P(),
        P(None, "chan"),
        P(None, "chan"),
        P("chan"),
        P(),
        P(),
        P("space", None),
        P("space", None),
        P("space"),
        P("space"),
        P("space"),
        P("space", None, None),
        P(None, "space", None),
        P(None, "space", None),
    )
    out_specs = (P("space", "chan"), P("space", None, "chan"))
    return jax.shard_map(shards, mesh=mesh, in_specs=in_specs, out_specs=out_specs, check_vma=False)
```

profile of v0, /device:TPU:1, one launch (start us, length us, event | category | flops | bytes accessed | tf_op | source)
XLA Modules:
  0.0 254.2 jit_solution(13938664651298129964)
XLA Ops:
  7.2 2.8 %fusion.68 = (bf16[1,720,512]{2,1,0:T(8,128)(2,1)}, bf16[720,512]{1,0:T(8,128)(2,1)S(1)}, bf16[1,720,512]{2,1,0:T(8,128)(2,1)}) fusion(bf16[3,720,512]{2,1,0:T(8,128)(2,1)} %param.24), kind=kLoop, calls=%fused_computation.122 | loop fusion | bytes 3686400 | tf_op jit(solution)/shard_map/slice | solution.py:14
  10.0 1.3 collective-permute-start.1
  11.3 5.5 %collective-permute-start = (bf16[1,720,512]{2,1,0:T(8,128)(2,1)}, bf16[1,720,512]{2,1,0:T(8,128)(2,1)}, u32[]{:S(2)}, u32[]{:S(2)}) collective-permute-start(bf16[1,720,512]{2,1,0:T(8,128)(2,1)} %get-tuple-element.12), channel_id=1, source_target_pairs={{0,4},{4,8},{8,12},{12,16},{16,20},{20,24},{24,28},{28,32},{32,36}... | collective-permute-start | bytes 2211848 | tf_op jit(solution)/shard_map/ppermute | solution.py:16
  17.8 2.8 %gather_fusion = bf16[720,512]{1,0:T(8,128)(2,1)S(1)} fusion(bf16[720,512]{1,0:T(8,128)(2,1)S(1)} %get-tuple-element.13, s32[1024]{0:T(1024)S(1)} %pad_clamp_fusion.3), kind=kCustom, calls=%fused_computation | custom fusion | bytes 1477440 | tf_op jit(solution)/shard_map/gather | solution.py:64
  20.7 0.6 compare_select_fusion.5
  21.3 6.8 %collective-permute-done.1 = bf16[1,720,512]{2,1,0:T(8,128)(2,1)} collective-permute-done((bf16[1,720,512]{2,1,0:T(8,128)(2,1)}, bf16[1,720,512]{2,1,0:T(8,128)(2,1)}, u32[]{:S(2)}, u32[]{:S(2)}) %collective-permute-start.1) | collective-permute-done | bytes 737312 | tf_op jit(solution)/shard_map/ppermute | solution.py:17
  28.1 1.2 bitcast_select_fusion
  29.3 3.5 %fusion.2 = (bf16[5,721,512]{2,1,0:T(8,128)(2,1)S(1)}, bf16[5,721,512]{2,1,0:T(8,128)(2,1)S(1)}) fusion(bf16[1,720,512]{2,1,0:T(8,128)(2,1)S(1)} %bitcast_select_fusion, bf16[3,720,512]{2,1,0:T(8,128)(2,1)S(1)} %copy-done.2, bf16[1,720,512]{2,1,0:T(8,128)(2,1)} %collective-permute-done), kind=kLoop, calls=%fused_computation.19 | loop fusion | flops 44298240 | bytes 11069440 | tf_op jit(solution)/shard_map/concatenate | solution.py:66
  32.8 2.3 fusion.66
  35.2 0.7 fusion.39
  35.9 1.5 pad_maximum_fusion.4
  37.4 0.7 convolution_add_fusion.8
  38.1 0.7 convolution_add_fusion.7
  38.9 0.7 convolution_add_fusion.6
  39.6 0.7 convolution_add_fusion.5
  40.4 0.7 convolution_add_fusion.4
  41.1 0.7 convolution_add_fusion.3
  41.8 0.7 convolution_add_fusion.2
  42.6 0.7 fusion.1
  43.4 1.7 fusion.13
  45.0 0.6 copy-done.5
  45.7 9.0 %all_gather.3 = bf16[160,512]{1,0:T(8,128)(2,1)S(1)} all-gather(bf16[160,128]{1,0:T(8,128)(2,1)S(1)} %fusion.13), channel_id=1, replica_groups=mesh['space'=64,'chan'=4] {'chan'}, dimensions={1}, use_global_device_ids=true | all-gather | bytes 204800 | tf_op jit(solution)/shard_map/all_gather | solution.py:87
  54.9 8.1 %gather_fusion.1 = bf16[2048,128]{1,0:T(8,128)(2,1)} fusion(bf16[160,128]{1,0:T(8,128)(2,1)S(1)} %convolution_convert_fusion.2, s32[2048]{0:T(1024)S(1)} %broadcast_clamp_fusion), kind=kCustom, calls=%fused_computation.1 | custom fusion | bytes 1056768 | tf_op jit(solution)/shard_map/gather | solution.py:93
  62.9 19.7 %all-to-all-start = ((bf16[64,32,128]{2,1,0:T(8,128)(2,1)}), bf16[64,32,128]{2,1,0:T(8,128)(2,1)S(1)}, u32[]{:S(2)}, u32[]{:S(2)}) async-start(bf16[64,32,128]{2,1,0:T(8,128)(2,1)} %bitcast.21), calls=%async_computation | async-start | bytes 1048576 | tf_op jit(solution)/shard_map/all_to_all | solution.py:94
  82.7 0.6 fusion.59
  83.4 0.7 reshape.229
  84.1 0.6 pad_clamp_fusion.2
  84.7 1.3 fusion.57
  86.1 1.3 fusion.58
  87.4 0.6 slice_bitcast_fusion.2
  88.0 1.1 fusion.70
  89.1 19.4 %gather_fusion.3 = f32[5120,128]{1,0:T(8,128)} fusion(f32[160,128]{1,0:T(8,128)S(1)} %fusion.70, s32[5120]{0:T(1024)} %fusion.58), kind=kCustom, calls=%fused_computation.3 | custom fusion | bytes 5263360 | tf_op jit(solution)/shard_map/gather | solution.py:96
  108.5 0.8 copy-done.3
  109.2 1.1 pad_maximum_fusion.6
  110.4 20.4 %gather_fusion.2 = bf16[5120,128]{1,0:T(8,128)(2,1)} fusion(bf16[2208,128]{1,0:T(8,128)(2,1)S(1)} %pad_maximum_fusion.6, s32[5120]{0:T(1024)} %fusion.57), kind=kCustom, calls=%fused_computation.2 | custom fusion | bytes 2641920 | tf_op jit(solution)/shard_map/gather | solution.py:96
  130.8 6.1 %fusion.16 = bf16[160,128]{1,0:T(8,128)(2,1)S(1)} fusion(bf16[5120,512]{1,0:T(8,128)(2,1)} %param.27, bf16[512,128]{1,0:T(8,128)(2,1)} %param.32, f32[5120,128]{1,0:T(8,128)} %gather_fusion.3, bf16[5120,128]{1,0:T(8,128)(2,1)} %gather_fusion.2, f32[128]{0:T(128)S(1)} %convert_element_type.76, s32[5120]{0:T(1024)S(1)} %copy-done.19, ...), kind=kOutput, calls=%fused_computation.40 | convolution fusion | flops 888197120 | bytes 9378304 | tf_op jit(solution)/shard_map/dot_general | solution.py:101
  136.9 0.9 convolution_convert_fusion.1
  137.9 0.2 fusion.69
  138.1 42.7 %all-reduce.3.cloned.1.call-done = bf16[160,512]{1,0:T(8,128)(2,1)} async-done(((bf16[160,512]{1,0:T(8,128)(2,1)}), bf16[160,512]{1,0:T(8,128)(2,1)}) %all-reduce.3.cloned.1.call-update) | async-done | bytes 163856 | tf_op jit(solution)/shard_map/psum | solution.py:27
  180.8 2.0 convolution_convert_fusion
  182.9 0.8 dynamic-slice
  183.7 42.5 %all-reduce.5.cloned.1.call-done = bf16[160,512]{1,0:T(8,128)(2,1)} async-done(((bf16[160,512]{1,0:T(8,128)(2,1)}), bf16[160,512]{1,0:T(8,128)(2,1)}) %all-reduce.5.cloned.1.call-update) | async-done | bytes 163856 | tf_op jit(solution)/shard_map/psum | solution.py:27
  226.2 1.0 convert_reduce_fusion
  227.3 1.1 multiply_reduce_fusion
  228.5 4.8 %gather_fusion.4 = bf16[2160,128]{1,0:T(8,128)(2,1)S(1)} fusion(bf16[160,128]{1,0:T(8,128)(2,1)S(1)} %fusion.54, s32[3072]{0:T(1024)S(1)} %copy-done.12), kind=kCustom, calls=%fused_computation.4 | custom fusion | bytes 1114560 | tf_op jit(solution)/shard_map/gather | solution.py:118
  233.3 5.6 %gather_fusion.5 = bf16[2160,128]{1,0:T(8,128)(2,1)} fusion(bf16[160,128]{1,0:T(8,128)(2,1)S(1)} %fusion.54, s32[3072]{0:T(1024)S(1)} %pad_clamp_fusion.1), kind=kCustom, calls=%fused_computation.5 | custom fusion | bytes 1114560 | tf_op jit(solution)/shard_map/gather | solution.py:118
  238.9 5.6 %gather_fusion.6 = bf16[2160,128]{1,0:T(8,128)(2,1)} fusion(bf16[160,128]{1,0:T(8,128)(2,1)S(1)} %fusion.54, s32[3072]{0:T(1024)S(1)} %pad_clamp_fusion), kind=kCustom, calls=%fused_computation.6 | custom fusion | bytes 1114560 | tf_op jit(solution)/shard_map/gather | solution.py:118
  244.5 2.8 %fusion.18 = bf16[3,720,128]{2,1,0:T(8,128)(2,1)} fusion(bf16[3,720,128]{2,1,0:T(8,128)(2,1)} %bitcast.103, bf16[3,720,128]{2,1,0:T(8,128)(2,1)} %bitcast.102, bf16[3,720,128]{2,1,0:T(8,128)(2,1)S(1)} %bitcast.101, f32[3,720]{1,0:T(4,128)S(1)} %copy-done.10, f32[3,720]{1,0:T(4,128)S(1)} %copy-done.11, f32[3,720]{1,0:T(4,128)S(1)} %copy-done.9, ...), kind=kLoop, calls=%fused_computation.44 | loop fusion | flops 3041280 | bytes 2790724 | tf_op jit(solution)/shard_map/convert_element_type | solution.py:121
  (83 shorter events, 1.1 us)
Async XLA Ops:
  7.2 129.8 %copy-start = (bf16[512,512]{1,0:T(8,128)(2,1)S(1)}, bf16[512,512]{1,0:T(8,128)(2,1)}, u32[]{:S(2)}) copy-start(bf16[512,512]{1,0:T(8,128)(2,1)} %param.34) | copy-start | bytes 1572868
  7.2 9.6 %copy-start.20 = (s32[1,64,32]{1,2,0:T(8,128)S(1)}, s32[1,64,32]{1,2,0:T(8,128)}, u32[]{:S(2)}) copy-start(s32[1,64,32]{1,2,0:T(8,128)} %param.45) | copy-start | bytes 24580
  7.2 9.5 %copy-start.24 = (s32[720]{0:T(1024)S(1)}, s32[720]{0:T(1024)}, u32[]{:S(2)}) copy-start(s32[720]{0:T(1024)} %param.25) | copy-start | bytes 8644
  7.2 9.6 %copy-start.27 = (bf16[128]{0:T(256)(128)(2,1)S(1)}, bf16[128]{0:T(256)(128)(2,1)}, u32[]{:S(2)}) copy-start(bf16[128]{0:T(256)(128)(2,1)} %param.29) | copy-start | bytes 772
  7.2 9.6 %copy-start.21 = (f32[3,720]{1,0:T(4,128)S(1)}, f32[3,720]{1,0:T(4,128)}, u32[]{:S(2)}) copy-start(f32[3,720]{1,0:T(4,128)} %param.41) | copy-start | bytes 25924
  7.2 9.7 %copy-start.22 = (s32[3,720]{1,0:T(4,128)S(1)}, s32[3,720]{1,0:T(4,128)}, u32[]{:S(2)}) copy-start(s32[3,720]{1,0:T(4,128)} %param.40) | copy-start | bytes 25924
  10.0 18.1 %collective-permute-start.1 = (bf16[1,720,512]{2,1,0:T(8,128)(2,1)}, bf16[1,720,512]{2,1,0:T(8,128)(2,1)}, u32[]{:S(2)}, u32[]{:S(2)}) collective-permute-start(bf16[1,720,512]{2,1,0:T(8,128)(2,1)} %get-tuple-element.14), channel_id=1, source_target_pairs={{4,0},{8,4},{12,8},{16,12},{20,16},{24,20},{28,24},{32,28},{36,32}... | collective-permute-start | bytes 2211848 | tf_op jit(solution)/shard_map/ppermute | solution.py:17
  11.3 18.0 %collective-permute-start = (bf16[1,720,512]{2,1,0:T(8,128)(2,1)}, bf16[1,720,512]{2,1,0:T(8,128)(2,1)}, u32[]{:S(2)}, u32[]{:S(2)}) collective-permute-start(bf16[1,720,512]{2,1,0:T(8,128)(2,1)} %get-tuple-element.12), channel_id=1, source_target_pairs={{0,4},{4,8},{8,12},{12,16},{16,20},{20,24},{24,28},{28,32},{32,36}... | collective-permute-start | bytes 2211848 | tf_op jit(solution)/shard_map/ppermute | solution.py:16
  17.8 2.9 %copy-start.17 = (s32[3,3,720]{2,1,0:T(4,128)S(1)}, s32[3,3,720]{2,1,0:T(4,128)}, u32[]{:S(2)}) copy-start(s32[3,3,720]{2,1,0:T(4,128)} %param.46) | copy-start | bytes 77764
  20.6 8.7 %copy-start.2 = (bf16[3,720,512]{2,1,0:T(8,128)(2,1)S(1)}, bf16[3,720,512]{2,1,0:T(8,128)(2,1)}, u32[]{:S(2)}) copy-start(bf16[3,720,512]{2,1,0:T(8,128)(2,1)} %param.24) | copy-start | bytes 6635524
  32.8 2.4 copy-start.4
  42.6 0.8 copy-start.26
  43.4 11.3 %copy-start.8 = (bf16[512,128]{1,0:T(8,128)(2,1)S(1)}, bf16[512,128]{1,0:T(8,128)(2,1)}, u32[]{:S(2)}) copy-start(bf16[512,128]{1,0:T(8,128)(2,1)} %param.30) | copy-start | bytes 393220
  45.0 0.6 copy-start.5
  54.8 28.5 %copy-start.28 = (bf16[128]{0:T(256)(128)(2,1)S(1)}, bf16[128]{0:T(256)(128)(2,1)}, u32[]{:S(2)}) copy-start(bf16[128]{0:T(256)(128)(2,1)} %param.33) | copy-start | bytes 772
  54.8 28.5 %copy-start.29 = (bf16[128]{0:T(256)(128)(2,1)S(1)}, bf16[128]{0:T(256)(128)(2,1)}, u32[]{:S(2)}) copy-start(bf16[128]{0:T(256)(128)(2,1)} %param.37) | copy-start | bytes 772
  54.9 28.5 %copy-start.15 = (s32[3,720,1]{1,0,2:T(4,128)S(1)}, s32[3,720,1]{1,0,2:T(4,128)}, u32[]{:S(2)}) copy-start(s32[3,720,1]{1,0,2:T(4,128)} %get-tuple-element.20) | copy-start | bytes 25924
  54.9 28.6 %copy-start.14 = (s32[3,720,1]{1,0,2:T(4,128)S(1)}, s32[3,720,1]{1,0,2:T(4,128)}, u32[]{:S(2)}) copy-start(s32[3,720,1]{1,0,2:T(4,128)} %get-tuple-element.22) | copy-start | bytes 25924
  54.9 32.5 %copy-start.18 = (f32[3,3,720]{2,1,0:T(4,128)S(1)}, f32[3,3,720]{2,1,0:T(4,128)}, u32[]{:S(2)}) copy-start(f32[3,3,720]{2,1,0:T(4,128)} %param.47) | copy-start | bytes 77764
  62.9 45.5 %all-to-all-start = ((bf16[64,32,128]{2,1,0:T(8,128)(2,1)}), bf16[64,32,128]{2,1,0:T(8,128)(2,1)S(1)}, u32[]{:S(2)}, u32[]{:S(2)}) async-start(bf16[64,32,128]{2,1,0:T(8,128)(2,1)} %bitcast.21), calls=%async_computation | async-start | bytes 1048576 | tf_op jit(solution)/shard_map/all_to_all | solution.py:94
  82.7 98.1 %all-reduce.3.cloned.1.call-start = ((), (), s32[]{:S(2)}) async-start(), calls=%async_computation.1 | async-start | bytes 327680 | tf_op jit(solution)/shard_map/psum | solution.py:27
  108.5 0.8 copy-start.3
  110.3 20.4 %copy-start.19 = (s32[5120]{0:T(1024)S(1)}, s32[5120]{0:T(1024)}, u32[]{:S(2)}) copy-start(s32[5120]{0:T(1024)} %param.43) | copy-start | bytes 61444
  110.3 20.4 %copy-start.23 = (bf16[5120]{0:T(1024)(128)(2,1)S(1)}, bf16[5120]{0:T(1024)(128)(2,1)}, u32[]{:S(2)}) copy-start(bf16[5120]{0:T(1024)(128)(2,1)} %fusion.59) | copy-start | bytes 30724
  130.8 7.1 %copy-start.7 = (bf16[512,128]{1,0:T(8,128)(2,1)S(1)}, bf16[512,128]{1,0:T(8,128)(2,1)}, u32[]{:S(2)}) copy-start(bf16[512,128]{1,0:T(8,128)(2,1)} %param.35) | copy-start | bytes 393220
  130.8 50.0 %copy-start.25 = (bf16[512,128]{1,0:T(8,128)(2,1)S(1)}, bf16[512,128]{1,0:T(8,128)(2,1)}, u32[]{:S(2)}) copy-start(bf16[512,128]{1,0:T(8,128)(2,1)} %param.36) | copy-start | bytes 393220
  130.8 52.0 %copy-start.16 = (s32[2160]{0:T(1024)S(1)}, s32[2160]{0:T(1024)}, u32[]{:S(2)}) copy-start(s32[2160]{0:T(1024)} %reshape.229) | copy-start | bytes 25924
  130.8 52.8 %copy-start.13 = (s32[3,720,1]{1,0,2:T(4,128)S(1)}, s32[3,720,1]{1,0,2:T(4,128)}, u32[]{:S(2)}) copy-start(s32[3,720,1]{1,0,2:T(4,128)} %get-tuple-element.21) | copy-start | bytes 25924
  136.9 91.5 %copy-start.6 = (bf16[160,128]{1,0:T(8,128)(2,1)S(1)}, bf16[160,128]{1,0:T(8,128)(2,1)}, u32[]{:S(2)}) copy-start(bf16[160,128]{1,0:T(8,128)(2,1)} %copy-done.5) | copy-start | bytes 122884
  136.9 91.6 %copy-start.12 = (s32[3072]{0:T(1024)S(1)}, s32[3072]{0:T(1024)}, u32[]{:S(2)}) copy-start(s32[3072]{0:T(1024)} %pad_clamp_fusion.2) | copy-start | bytes 36868
  137.8 88.4 %all-reduce.5.cloned.1.call-start = ((), (), s32[]{:S(2)}) async-start(), calls=%async_computation.2 | async-start | bytes 327680 | tf_op jit(solution)/shard_map/psum | solution.py:27
  228.5 10.4 %copy-start.1 = (bf16[160,128]{1,0:T(8,128)(2,1)}, bf16[160,128]{1,0:T(8,128)(2,1)S(1)}, u32[]{:S(2)}) copy-start(bf16[160,128]{1,0:T(8,128)(2,1)S(1)} %fusion.54) | copy-start | bytes 122884
  238.9 5.6 %copy-start.9 = (f32[3,720]{1,0:T(4,128)S(1)}, f32[3,720]{1,0:T(4,128)}, u32[]{:S(2)}) copy-start(f32[3,720]{1,0:T(4,128)} %get-tuple-element.17) | copy-start | bytes 25924
  238.9 5.6 %copy-start.10 = (f32[3,720]{1,0:T(4,128)S(1)}, f32[3,720]{1,0:T(4,128)}, u32[]{:S(2)}) copy-start(f32[3,720]{1,0:T(4,128)} %get-tuple-element.18) | copy-start | bytes 25924
  238.9 5.6 %copy-start.11 = (f32[3,720]{1,0:T(4,128)S(1)}, f32[3,720]{1,0:T(4,128)}, u32[]{:S(2)}) copy-start(f32[3,720]{1,0:T(4,128)} %get-tuple-element.19) | copy-start | bytes 25924
Sparse Core Ops, SparseCore 0:
  138.0 42.8 all-reduce.2
  184.2 41.9 all-reduce.4
where the time goes:
time: 256 us; the launch traced here: 254 us
  waiting for transfers between devices  92.1 us (36%)
  local copies, waits for them, and re-layouts  75.8 us (30%)
  starting transfers between devices  26.6 us (10%)
  matrix products  18.7 us (7%)
  other arithmetic  16.8 us (7%)
  between operations  15.2 us (6%)
  blocking collectives  8.98 us (4%)
    psum x2, waiting for transfers between devices, project_rows(): lax.psum(partial_sum.astype(jnp.bfloat16), 'chan').astype(jnp.float32)  85.2 us
    gather x1, local copies, waits for them, and re-layouts, shards(): source_table[edge_source].astype(jnp.float32) + recv[edge_target]  20.4 us
    all_to_all x1, starting transfers between devices, shards(): lax.all_to_all(outgoing, 'space', split_axis=0, concat_axis=0, tiled=True)  19.7 us
    gather x1, local copies, waits for them, and re-layouts, shards(): recv[edge_target]  19.4 us
    gather x3, local copies, waits for them, and re-layouts, shards(): node_out[read_node[corner]].astype(jnp.float32)  16 us
    all_gather x1, blocking collectives, shards(): nodes = lax.all_gather(nodes_part, 'chan', axis=1, tiled=True)  8.98 us
    gather x1, local copies, waits for them, and re-layouts, shards(): outgoing = sent[send_rows[0]]  8.05 us
    ppermute x1, waiting for transfers between devices, with_halo(): after = lax.ppermute(leading, axis, down)  6.8 us
  transfers between devices with their start and end apart: 5, of which 3 were waited for; matrix products, arithmetic and copies ran while one was open for 12% of the time, Pallas kernels for 0%

commit v1 on v0

v1 whole, which is shorter than its diff:
```python
import jax
import jax.numpy as jnp
from jax import lax
from jax.experimental import pallas as pl
from jax.experimental.pallas import tpu as pltpu
from jax.sharding import PartitionSpec as P

f32 = jnp.float32
bf16 = jnp.bfloat16
i32 = jnp.int32
norm_eps = 1e-05
MESH = pl.DeviceIdType.MESH

SPACE, CHAN = 64, 4
NY, NZ, NX = 2, 8, 4
FEAT, COLS = 512, 128
BAND, LON = 3, 720
NODES = 160
EDGES = 5120
CAP = 32
MCH = 240
LONP = 768
SHIFTS = (4, 0, 3, 5, 2, 6, 1, 7)


def dot(a, b):
    return jnp.dot(a, b, preferred_element_type=f32)


def silu(v):
    return 0.5 * v * (1.0 + jnp.tanh(0.5 * v))


def kernel(
    grid_h, fold_h, mesh_h, edge_h, convw_h, convb_h, srcw_h, tgtw_h, edgew_h, edgeb_h,
    msgw_h, selfw_h, inw_h, nodeb_h, outw_h, gain_h, celln_h, cellw_h, esrc_h, etgt_h,
    ecount, send_h, readn_h, readw_h,
    node_out, grid_out,
    x, fold, mesh_v, edge, wcat, convb, srcw, tgtw, edgew, edgeb,
    msgw, selfw, inw, nodeb, outw, gain, celln, cellw, esrc, etgt, sendr, readn, readw,
    z, cpart, halo_out, halo_in, act, inc_a, sel_o, outg, table, nodes4, pool4, hid4,
    onehot, half_b, pool_p, acc1, acc2, incoming, ridx, rwt, rmat, upd, srcc,
    load_sem, halo_send, halo_recv, gat_send, gat_recv, a2a_send, a2a_recv,
):
    me = lax.axis_index("space")
    ch = lax.axis_index("chan")
    my, mz, mx = me // 32, (me // 4) % 8, me % 4

    loads = {}

    def load(name, src, dst):
        k = len(loads)
        c = pltpu.make_async_copy(src, dst, load_sem.at[k])
        c.start()
        loads[name] = c

    def ready(*names):
        for name in names:
            loads[name].wait()

    def load_w(a):
        for b in range(3):
            load(("w", a, b), convw_h.at[a, b], wcat.at[a, :, b * COLS:(b + 1) * COLS])

    load("x0", grid_h.at[0], x.at[0])
    load_w(2)
    load("x2", grid_h.at[2], x.at[2])
    load_w(0)
    load("x1", grid_h.at[1], x.at[1])
    load_w(1)
    for name, s, d in (
        ("convb", convb_h, convb), ("celln", celln_h, celln), ("cellw", cellw_h, cellw),
        ("sendr", send_h.at[0], sendr), ("esrc", esrc_h, esrc), ("etgt", etgt_h, etgt),
        ("fold", fold_h, fold), ("mesh", mesh_h, mesh_v), ("srcw", srcw_h, srcw), ("tgtw", tgtw_h, tgtw),
        ("edgew", edgew_h, edgew), ("edgeb", edgeb_h, edgeb),
        ("e0", edge_h.at[0:2560], edge.at[0:2560]), ("e1", edge_h.at[2560:5120], edge.at[2560:5120]),
        ("selfw", selfw_h, selfw), ("msgw", msgw_h, msgw), ("inw", inw_h, inw), ("nodeb", nodeb_h, nodeb),
        ("outw", outw_h, outw), ("gain", gain_h, gain), ("readn", readn_h, readn), ("readw", readw_h, readw),
    ):
        load(name, s, d)

    barrier = pltpu.get_barrier_semaphore()

    def greet(d, _):
        pl.semaphore_signal(barrier, inc=1, device_id={"space": (me + d) % SPACE}, device_id_type=MESH)
        return 0

    lax.fori_loop(1, SPACE, greet, 0)
    for d in range(1, CHAN):
        pl.semaphore_signal(barrier, inc=1, device_id={"chan": (ch + d) % CHAN}, device_id_type=MESH)

    def conv_z(terms):
        for m in range(LON // MCH):
            rows = pl.ds(m * MCH, MCH)
            acc = None
            for xr, a in terms:
                d = dot(xr[rows, :], wcat[a])
                acc = d if acc is None else acc + d
            z[pl.ds(8 + m * MCH, MCH), :] = acc
        z[7:8, 0:COLS] = z[LON + 7:LON + 8, 0:COLS]
        z[LON + 8:LON + 9, 2 * COLS:3 * COLS] = z[8:9, 2 * COLS:3 * COLS]

    def shifted(m):
        o = m * MCH
        return (
            z[pl.ds(o + 7, MCH), 0:COLS]
            + z[pl.ds(o + 8, MCH), COLS:2 * COLS]
            + z[pl.ds(o + 9, MCH), 2 * COLS:3 * COLS]
        )

    chunks = range(LON // MCH)

    ready("x0", ("w", 2, 0), ("w", 2, 1), ("w", 2, 2))
    conv_z([(x.at[0], 2)])
    for m in chunks:
        halo_out[0, pl.ds(m * MCH, MCH), :] = shifted(m).astype(bf16)
    pl.semaphore_wait(barrier, SPACE - 1 + CHAN - 1)

    def halo_copy(k):
        peer = (me + SPACE - 1) % SPACE if k == 0 else (me + 1) % SPACE
        return pltpu.make_async_remote_copy(
            src_ref=halo_out.at[k], dst_ref=halo_in.at[k], send_sem=halo_send.at[k], recv_sem=halo_recv.at[k],
            device_id={"space": peer}, device_id_type=MESH,
        )

    halo = [halo_copy(0), halo_copy(1)]
    halo[0].start()
    ready("x2", ("w", 0, 0), ("w", 0, 1), ("w", 0, 2))
    conv_z([(x.at[2], 0)])
    for m in chunks:
        halo_out[1, pl.ds(m * MCH, MCH), :] = shifted(m).astype(bf16)
    halo[1].start()

    ready("x1", ("w", 1, 0), ("w", 1, 1), ("w", 1, 2), "convb", "celln", "cellw")
    bias = convb[...].astype(f32)
    for r, terms in (
        (0, [(x.at[0], 1), (x.at[1], 2)]),
        (2, [(x.at[1], 0), (x.at[2], 1)]),
        (1, [(x.at[0], 0), (x.at[1], 1), (x.at[2], 2)]),
    ):
        conv_z(terms)
        for m in chunks:
            v = shifted(m) + bias
            rows = pl.ds(m * MCH, MCH)
            if r == 1:
                act[1, rows, :] = silu(v).astype(bf16)
            else:
                cpart[r // 2, rows, :] = v

    ready("fold")

    @pl.when(me == SPACE - 1)
    def _():
        def body(t, _):
            rows = pl.ds(pl.multiple_of(t * 16, 16), 16)
            ids = lax.broadcasted_iota(i32, (16, LON), 0) + t * 16
            pick = jnp.where(ids == fold[...], 1.0, 0.0).astype(bf16)
            srcc[rows, :] = pick
            return 0

        lax.fori_loop(0, LON // 16, body, 0)
        xf = lax.dot_general(srcc[...], x[2], (((0,), (0,)), ((), ())), preferred_element_type=f32)
        upd_x = xf.astype(bf16)
        onehot[0:LON, 0:FEAT] = upd_x
        conv_z([(onehot.at[0:LON, 0:FEAT], 2)])
        for m in chunks:
            rows = pl.ds(m * MCH, MCH)
            cpart[1, rows, :] = cpart[1, rows, :] + shifted(m)

    for r in range(BAND):
        ids = lax.broadcasted_iota(i32, (NODES, LON), 0)
        inc_a[r] = jnp.where(ids == celln[r:r + 1, :], cellw[r:r + 1, :], 0.0).astype(bf16)

    ready("sendr", "esrc", "etgt")
    send_t = sendr[...].astype(f32).T
    lane256 = lax.broadcasted_iota(i32, (CAP, 256), 1).astype(f32)
    for p in range(SPACE):
        sel_o[p * CAP:(p + 1) * CAP, :] = jnp.where(send_t[:, p:p + 1] == lane256, 1.0, 0.0).astype(bf16)

    s = esrc[...]
    u = s - NODES
    q = lax.shift_right_logical(u, 5) & 63
    k = u & 31
    dz = (mz - (lax.shift_right_logical(q, 2) & 7)) & 7
    dy = (my - lax.shift_right_logical(q, 5)) & 1
    dx = (mx - (q & 3)) & 3
    t = jnp.zeros_like(s)
    for pos, shift in enumerate(SHIFTS):
        t = jnp.where(dz == shift, pos, t)
    remote = 256 + lax.shift_right_logical(t, 1) * 256 + (dy * 4 + dx) * CAP + k
    col = jnp.where(u < 0, s, remote)
    halfbit = jnp.where(u < 0, 0, t & 1)
    slot = lax.broadcasted_iota(i32, s.shape, 0) * 128 + lax.broadcasted_iota(i32, s.shape, 1)
    live_t = jnp.where(slot < ecount[0], etgt[...], -1)
    srcc2 = col + 2048 * halfbit
    ridx[0] = srcc2
    ridx[1] = etgt[...]
    ridx[2] = live_t

    lane_f = lax.broadcasted_iota(i32, (128, 128), 1).astype(f32)

    def column(which, e):
        row = ridx[which, pl.ds(e, 1), :].astype(f32)
        return jnp.broadcast_to(row, (128, 128)).T

    def build(e, _):
        rows = pl.ds(pl.multiple_of(e * 128, 128), 128)
        c = column(0, e)
        hb = jnp.where(c >= 2048.0, 1.0, 0.0)
        half_b[rows, :] = hb.astype(bf16)
        c = c - 2048.0 * hb
        hi = jnp.floor(c * (1.0 / 128.0))
        lo = c - 128.0 * hi
        m = jnp.where(lo == lane_f, hi, -1.0).astype(bf16)
        one = jnp.ones((128, 128), bf16)
        zero = jnp.zeros((128, 128), bf16)
        for tile in range(10):
            at = tile if tile < 2 else tile + 2
            onehot[rows, at * 128:(at + 1) * 128] = jnp.where(m == jnp.asarray(tile, bf16), one, zero)
        c = column(1, e)
        for tile in range(2):
            onehot[rows, (2 + tile) * 128:(3 + tile) * 128] = jnp.where(
                c == lane_f + 128.0 * tile, 1.0, 0.0
            ).astype(bf16)
        ids = lax.broadcasted_iota(i32, (NODES, 128), 0)
        pool_p[:, rows] = jnp.where(ids == ridx[2, pl.ds(e, 1), :], 1.0, 0.0).astype(bf16)
        return 0

    FIRST = 20
    lax.fori_loop(0, FIRST, build, 0)

    halo[0].wait_recv()
    halo[1].wait_recv()
    south_ok = jnp.where(me > 0, 1.0, 0.0)
    north_ok = jnp.where(me < SPACE - 1, 1.0, 0.0)
    for m in chunks:
        rows = pl.ds(m * MCH, MCH)
        act[0, rows, :] = silu(cpart[0, rows, :] + halo_in[1, rows, :].astype(f32) * south_ok).astype(bf16)
        act[2, rows, :] = silu(cpart[1, rows, :] + halo_in[0, rows, :].astype(f32) * north_ok).astype(bf16)
    ready("mesh")
    agg = dot(inc_a[0], act[0]) + dot(inc_a[1], act[1]) + dot(inc_a[2], act[2])
    mine = (mesh_v[...].astype(f32) + agg).astype(bf16)

    def gather_start(buf, stage):
        out = []
        for d in range(1, CHAN):
            c = pltpu.make_async_remote_copy(
                src_ref=buf.at[ch], dst_ref=buf.at[ch],
                send_sem=gat_send.at[stage, d], recv_sem=gat_recv.at[stage, d],
                device_id={"chan": (ch + d) % CHAN}, device_id_type=MESH,
            )
            c.start()
            out.append(c)
        return out

    def gathered(buf):
        return jnp.concatenate([buf[0], buf[1], buf[2], buf[3]], axis=1)

    nodes4[ch] = mine
    g_nodes = gather_start(nodes4, 0)
    ready("srcw", "tgtw")
    lax.fori_loop(FIRST, FIRST + 4, build, 0)
    for c in g_nodes:
        c.wait_recv()
    nodes = gathered(nodes4)
    sent = dot(nodes, srcw[...]).astype(bf16)
    table[...] = jnp.zeros_like(table)
    table[0:NODES, :] = sent
    for b in range(SPACE * CAP // 256):
        picked = dot(sel_o[b * 256:(b + 1) * 256, :], table[0:256, :]).astype(bf16)
        outg[b * 8:(b + 1) * 8] = picked.reshape(8, CAP, COLS)

    def a2a_copy(pos, j):
        peer = ((my + j // 4) % NY) * 32 + ((mz + SHIFTS[pos]) % NZ) * 4 + (mx + j % 4) % NX
        sl = pos * 8 + j
        return pltpu.make_async_remote_copy(
            src_ref=outg.at[peer], dst_ref=incoming.at[sl], send_sem=a2a_send.at[sl], recv_sem=a2a_recv.at[sl],
            device_id={"space": peer}, device_id_type=MESH,
        )

    for pos in range(8):
        def go(j, _, pos=pos):
            a2a_copy(pos, j).start()
            return 0
        lax.fori_loop(1 if SHIFTS[pos] == 0 else 0, 8, go, 0)
    incoming[8] = outg[me]

    table[256:256 + NODES, :] = dot(nodes, tgtw[...]).astype(bf16)
    lax.fori_loop(FIRST + 4, EDGES // 128, build, 0)
    ready("edgew", "edgeb", "e0", "e1")
    ebias = edgeb[...].astype(f32)

    def own(e, _):
        rows = pl.ds(pl.multiple_of(e * 256, 256), 256)
        acc1[rows, :] = dot(edge[rows, :], edgew[...]) + dot(onehot[rows, 0:512], table[...]) + ebias
        return 0

    lax.fori_loop(0, EDGES // 256, own, 0)

    ready("selfw", "nodeb", "readn", "readw", "msgw", "inw", "outw", "gain")
    self_part = dot(nodes, selfw[...]) + nodeb[...].astype(f32)
    ids = lax.broadcasted_iota(i32, (NODES, LON), 0)
    for r in range(BAND):
        w = jnp.zeros((NODES, LON), f32)
        for corner in range(3):
            w = w + jnp.where(ids == readn[corner, r:r + 1, :], readw[corner, r:r + 1, :], 0.0)
        rwt[:, 0:LON] = w
        rwt[:, LON:LONP] = jnp.zeros((NODES, LONP - LON), f32)
        for tile in range(LONP // 128):
            rmat[r, tile * 128:(tile + 1) * 128, :] = rwt[:, tile * 128:(tile + 1) * 128].T.astype(bf16)

    def group_table(g):
        left = incoming[16 * g:16 * g + 8].reshape(256, COLS)
        right = incoming[16 * g + 8:16 * g + 16].reshape(256, COLS)
        return jnp.concatenate([left, right], axis=1)

    def arrive(g):
        for pos in (2 * g, 2 * g + 1):
            def got(j, _, pos=pos):
                a2a_copy(pos, j).wait_recv()
                return 0
            lax.fori_loop(1 if SHIFTS[pos] == 0 else 0, 8, got, 0)

    for g in range(3):
        arrive(g)
        tg = group_table(g)

        def remote_part(e, _, g=g, tg=tg):
            rows = pl.ds(pl.multiple_of(e * 256, 256), 256)
            d = dot(onehot[rows, 512 + 256 * g:768 + 256 * g], tg)
            acc2[rows, :] = d if g == 0 else acc2[rows, :] + d
            return 0

        lax.fori_loop(0, EDGES // 256, remote_part, 0)
    arrive(3)
    tg = group_table(3)

    def finish(e, pooled):
        rows = pl.ds(pl.multiple_of(e * 256, 256), 256)
        d = dot(onehot[rows, 1280:1536], tg) + acc2[rows, :]
        pre = acc1[rows, :] + jnp.where(half_b[rows, :].astype(f32) > 0.5, d[:, COLS:], d[:, :COLS])
        return pooled + dot(pool_p[:, rows], silu(pre).astype(bf16))

    pooled = lax.fori_loop(0, EDGES // 256, finish, jnp.zeros((NODES, COLS), f32))
    pool4[ch] = pooled.astype(bf16)
    g_pool = gather_start(pool4, 1)
    for c in g_pool:
        c.wait_recv()
    message = dot(gathered(pool4), msgw[...]).astype(bf16)
    hid4[ch] = silu(self_part + dot(message, inw[...])).astype(bf16)
    g_hid = gather_start(hid4, 2)
    for c in g_hid:
        c.wait_recv()
    update = dot(gathered(hid4), outw[...])
    mean = jnp.mean(update, axis=1, keepdims=True)
    centred = update - mean
    var = jnp.mean(jnp.square(centred), axis=1, keepdims=True)
    upd[...] = gain[...] * centred * lax.rsqrt(var + norm_eps)
    own_cols = pl.ds(pl.multiple_of(ch * COLS, COLS), COLS)
    result = (mine.astype(f32) + upd[:, own_cols]).astype(bf16)
    node_out[...] = result
    for r in range(BAND):
        for m in chunks:
            rows = pl.ds(m * MCH, MCH)
            got = dot(rmat[r, rows, :], result)
            grid_out[r, rows, :] = (x[r, rows, own_cols].astype(f32) + got).astype(bf16)

    halo[0].wait_send()
    halo[1].wait_send()
    for c in g_nodes + g_pool + g_hid:
        c.wait_send()
    for pos in range(8):
        def left(j, _, pos=pos):
            a2a_copy(pos, j).wait_send()
            return 0
        lax.fori_loop(1 if SHIFTS[pos] == 0 else 0, 8, left, 0)


def shards(*args):
    (grid_state, fold_columns, mesh_state, edge_state, conv_weight, conv_bias, source_weight, target_weight,
     edge_weight, edge_bias, message_weight, self_weight, inbox_weight, node_bias, output_weight, output_gain,
     cell_node, cell_weight, edge_source, edge_target, edge_count, send_rows, read_node, read_weight) = args
    anyspace = pl.BlockSpec(memory_space=pl.ANY)
    vmem = pl.BlockSpec(memory_space=pltpu.VMEM)
    V = pltpu.VMEM
    in_specs = [anyspace] * 24
    in_specs[20] = pl.BlockSpec(memory_space=pltpu.SMEM)
    return pl.pallas_call(
        kernel,
        out_shape=(
            jax.ShapeDtypeStruct((NODES, COLS), bf16),
            jax.ShapeDtypeStruct((BAND, LON, COLS), bf16),
        ),
        in_specs=in_specs,
        out_specs=(vmem, vmem),
        scratch_shapes=[
            V((BAND, LON, FEAT), bf16), V((1, LON), i32), V((NODES, COLS), bf16), V((EDGES, FEAT), bf16),
            V((3, FEAT, 3 * COLS), bf16), V((1, COLS), bf16), V((FEAT, COLS), bf16), V((FEAT, COLS), bf16),
            V((FEAT, COLS), bf16), V((1, COLS), bf16),
            V((FEAT, FEAT), bf16), V((FEAT, COLS), bf16), V((FEAT, COLS), bf16), V((1, COLS), bf16),
            V((FEAT, FEAT), bf16), V((1, FEAT), f32), V((BAND, LON), i32), V((BAND, LON), f32),
            V((40, 128), i32), V((40, 128), i32), V((SPACE, CAP), i32), V((3, BAND, LON), i32), V((3, BAND, LON), f32),
            V((LON + 16, 3 * COLS), f32), V((2, LON, COLS), f32), V((2, LON, COLS), bf16), V((2, LON, COLS), bf16),
            V((BAND, LON, COLS), bf16), V((BAND, NODES, LON), bf16), V((SPACE * CAP, 256), bf16),
            V((SPACE, CAP, COLS), bf16), V((512, COLS), bf16),
            V((CHAN, NODES, COLS), bf16), V((CHAN, NODES, COLS), bf16), V((CHAN, NODES, COLS), bf16),
            V((EDGES, 1536), bf16), V((EDGES, 128), bf16), V((NODES, EDGES), bf16),
            V((EDGES, COLS), f32), V((EDGES, 2 * COLS), f32), V((SPACE, CAP, COLS), bf16),
            V((3, 40, 128), i32), V((NODES, LONP), f32), V((BAND, LONP, NODES), bf16), V((NODES, FEAT), f32),
            V((LON, LON), bf16),
            pltpu.SemaphoreType.DMA((40,)), pltpu.SemaphoreType.DMA((2,)), pltpu.SemaphoreType.DMA((2,)),
            pltpu.SemaphoreType.DMA((3, CHAN)), pltpu.SemaphoreType.DMA((3, CHAN)),
            pltpu.SemaphoreType.DMA((SPACE,)), pltpu.SemaphoreType.DMA((SPACE,)),
        ],
        compiler_params=pltpu.CompilerParams(
            collective_id=0, has_side_effects=True, vmem_limit_bytes=60 * 1024 * 1024
        ),
    )(
        grid_state, fold_columns.reshape(1, LON), mesh_state, edge_state, conv_weight, conv_bias.reshape(1, COLS),
        source_weight, target_weight, edge_weight, edge_bias.reshape(1, COLS), message_weight, self_weight,
        inbox_weight, node_bias.reshape(1, COLS), output_weight, output_gain.reshape(1, FEAT), cell_node, cell_weight,
        edge_source.reshape(40, 128), edge_target.reshape(40, 128), edge_count, send_rows, read_node, read_weight,
    )


def solution(mesh):
    in_specs = (
        P("space", None, None), P(), P("space", "chan"), P("space", None), P(None, None, None, "chan"), P("chan"),
        P(None, "chan"), P(None, "chan"), P(None, "chan"), P("chan"), P(), P(None, "chan"), P(None, "chan"), P("chan"),
        P(), P(), P("space", None), P("space", None), P("space"), P("space"), P("space"), P("space", None, None),
        P(None, "space", None), P(None, "space", None),
    )
    out_specs = (P("space", "chan"), P("space", None, "chan"))
    return jax.shard_map(shards, mesh=mesh, in_specs=in_specs, out_specs=out_specs, check_vma=False)
```

time: 256 us -> 74.5 us (0.29)
  waiting for transfers between devices: 92.1 us -> 0 us
  local copies, waits for them, and re-layouts: 75.8 us -> 5.97 us
  Pallas kernels: 0 us -> 66.9 us
  starting transfers between devices: 26.6 us -> 0 us
  matrix products: 18.7 us -> 0 us
  other arithmetic: 16.8 us -> 0 us
  between operations: 15.2 us -> 1.29 us
  blocking collectives: 8.98 us -> 0 us
    psum x2 -> x0, waiting for transfers between devices: 85.2 us -> none  [project_rows(): lax.psum(partial_sum.astype(jnp.bfloat16), 'chan').astype(jnp.float32)]
    pallas_call x0 -> x1, Pallas kernels: none -> 66.9 us  [shards(): pl.pallas_call(kernel, out_shape=(jax.ShapeDtypeStruct((NODES, COLS), bf1...]
    gather x7 -> x0, local copies, waits for them, and re-layouts: 66.6 us -> none  [the longest x1 20.4 us: shards(): source_table[edge_source].astype(jnp.float32) + recv[edge_target]]
    all_to_all x1 -> x0, starting transfers between devices: 19.7 us -> none  [shards(): lax.all_to_all(outgoing, 'space', split_axis=0, concat_axis=0, tiled=True)]
    dot_general x16 -> x0, matrix products: 18.7 us -> none  [the longest x9 6.61 us: shards(): jnp.dot(window, conv_weight[shift_row, shift_col], preferred_element_type...]
    all_gather x1 -> x0, blocking collectives: 8.98 us -> none  [shards(): nodes = lax.all_gather(nodes_part, 'chan', axis=1, tiled=True)]
    ppermute x2 -> x0, waiting for transfers between devices: 6.8 us -> none  [the longest x1 6.8 us: with_halo(): after = lax.ppermute(leading, axis, down)]
    ppermute x2 -> x0, starting transfers between devices: 6.73 us -> none  [the longest x1 5.45 us: with_halo(): before = lax.ppermute(last, axis, up)]
  transfers between devices with their start and end apart: 5 -> 0, of which waited for: 3 -> 0; matrix products, arithmetic and copies ran while one was open for 12% -> 0% of each run, Pallas kernels for 0% -> 0%
where the time goes in v1:
time: 74.5 us; the launch traced here: 74.2 us
  Pallas kernels  66.9 us (90%)
  local copies, waits for them, and re-layouts  5.97 us (8%)
  between operations  1.29 us (2%)
    pallas_call x1, Pallas kernels, shards(): pl.pallas_call(kernel, out_shape=(jax.ShapeDtypeStruct((NODES, COLS), bf1...  66.9 us
    unnamed x3, local copies, waits for them, and re-layouts  4.7 us

profile of v1, /device:TPU:1, one launch (start us, length us, event | category | flops | bytes accessed | tf_op | source)
XLA Modules:
  0.0 74.2 jit_solution(2554675673198611235)
XLA Ops:
  1.3 1.3 %reshape.25.fold_h = s32[1,720]{1,0:T(1,128)} reshape(s32[720]{0:T(1024)} %param.25) | data formatting | bytes 5760 | tf_op jit(solution)/shard_map/reshape | solution.py:419
  2.5 1.4 %copy.26.send_h = s32[1,64,32]{2,1,0:T(8,128)} copy(s32[1,64,32]{1,2,0:T(8,128)} %param.45) | data formatting | bytes 16384 | tf_op args[21]
  4.0 66.9 %shard_map.239 = (bf16[160,128]{1,0:T(8,128)(2,1)}, bf16[3,720,128]{2,1,0:T(8,128)(2,1)}) custom-call(bf16[3,720,512]{2,1,0:T(8,128)(2,1)} %grid_h.1, s32[1,720]{1,0:T(1,128)} %reshape.25.fold_h, bf16[160,128]{1,0:T(8,128)(2,1)} %mesh_h.1, bf16[5120,512]{1,0:T(8,128)(2,1)} %edge_h.1, bf16[3,3,512,128]{3,2,1,0:T(8,128)(2,1)} %convw_h.1, ...), custom_call_target="tpu_custom_call" | custom-call | tf_op jit(solution)/shard_map/pallas_call | solution.py:388
  70.9 1.4 %copy.30 = bf16[160,128]{1,0:T(8,128)(2,1)} copy(bf16[160,128]{1,0:T(8,128)(2,1)} %get-tuple-element.4) | data formatting | bytes 81920
  72.3 1.9 %copy.31 = bf16[3,720,128]{2,1,0:T(8,128)(2,1)} copy(bf16[3,720,128]{2,1,0:T(8,128)(2,1)} %get-tuple-element.5) | data formatting | bytes 1105920

commit v2 on v1

--- a/solution.py
+++ b/solution.py
@@ -20,7 +20,9 @@
 CAP = 32
 MCH = 240
 LONP = 768
-SHIFTS = (4, 0, 3, 5, 2, 6, 1, 7)
+SHIFTS = (0, 4, 3, 5, 2, 6, 1, 7)
+ECH = 1280
+UNROLL = 4
 
 
 def dot(a, b):
@@ -35,12 +37,12 @@
     grid_h, fold_h, mesh_h, edge_h, convw_h, convb_h, srcw_h, tgtw_h, edgew_h, edgeb_h,
     msgw_h, selfw_h, inw_h, nodeb_h, outw_h, gain_h, celln_h, cellw_h, esrc_h, etgt_h,
     ecount, send_h, readn_h, readw_h,
-    node_out, grid_out,
+    node_out, rmat_h,
     x, fold, mesh_v, edge, wcat, convb, srcw, tgtw, edgew, edgeb,
     msgw, selfw, inw, nodeb, outw, gain, celln, cellw, esrc, etgt, sendr, readn, readw,
     z, cpart, halo_out, halo_in, act, inc_a, sel_o, outg, table, nodes4, pool4, hid4,
     onehot, half_b, pool_p, acc1, acc2, incoming, ridx, rwt, rmat, upd, srcc,
-    load_sem, halo_send, halo_recv, gat_send, gat_recv, a2a_send, a2a_recv,
+    load_sem, halo_send, halo_recv, gat_send, gat_recv, a2a_send, a2a_recv, rmat_sem, near_sem,
 ):
     me = lax.axis_index("space")
     ch = lax.axis_index("chan")
@@ -64,6 +66,24 @@
 
     load("x0", grid_h.at[0], x.at[0])
     load_w(2)
+
+    barrier = pltpu.get_barrier_semaphore()
+
+    def hail(sem, **where):
+        pl.semaphore_signal(sem, inc=1, device_id=where, device_id_type=MESH)
+
+    def at(dy, dz, dx):
+        return ((my + dy) % NY) * 32 + ((mz + dz) % NZ) * 4 + (mx + dx) % NX
+
+    hail(barrier, space=(me + 1) % SPACE)
+    hail(barrier, space=(me + SPACE - 1) % SPACE)
+    for d in range(1, CHAN):
+        hail(barrier, chan=(ch + d) % CHAN)
+    hail(barrier, space=at(1, 0, 0))
+    for d in range(1, NX):
+        hail(barrier, space=at(0, 0, d))
+    for d in range(1, NZ):
+        hail(barrier, space=at(0, d, 0))
     load("x2", grid_h.at[2], x.at[2])
     load_w(0)
     load("x1", grid_h.at[1], x.at[1])
@@ -79,16 +99,6 @@
     ):
         load(name, s, d)
 
-    barrier = pltpu.get_barrier_semaphore()
-
-    def greet(d, _):
-        pl.semaphore_signal(barrier, inc=1, device_id={"space": (me + d) % SPACE}, device_id_type=MESH)
-        return 0
-
-    lax.fori_loop(1, SPACE, greet, 0)
-    for d in range(1, CHAN):
-        pl.semaphore_signal(barrier, inc=1, device_id={"chan": (ch + d) % CHAN}, device_id_type=MESH)
-
     def conv_z(terms):
         for m in range(LON // MCH):
             rows = pl.ds(m * MCH, MCH)
@@ -114,7 +124,9 @@
     conv_z([(x.at[0], 2)])
     for m in chunks:
         halo_out[0, pl.ds(m * MCH, MCH), :] = shifted(m).astype(bf16)
-    pl.semaphore_wait(barrier, SPACE - 1 + CHAN - 1)
+    pl.semaphore_wait(barrier, 2 + CHAN - 1 + NY - 1 + NX - 1 + NZ - 1)
+    for d in range(1, NX):
+        hail(near_sem.at[0], space=at(0, 0, d))
 
     def halo_copy(k):
         peer = (me + SPACE - 1) % SPACE if k == 0 else (me + 1) % SPACE
@@ -130,6 +142,8 @@
     for m in chunks:
         halo_out[1, pl.ds(m * MCH, MCH), :] = shifted(m).astype(bf16)
     halo[1].start()
+    pl.semaphore_wait(near_sem.at[0], NX - 1)
+    hail(near_sem.at[1], space=at(1, 0, 0))
 
     ready("x1", ("w", 1, 0), ("w", 1, 1), ("w", 1, 2), "convb", "celln", "cellw")
     bias = convb[...].astype(f32)
@@ -154,7 +168,7 @@
         def body(t, _):
             rows = pl.ds(pl.multiple_of(t * 16, 16), 16)
             ids = lax.broadcasted_iota(i32, (16, LON), 0) + t * 16
-            pick = jnp.where(ids == fold[...], 1.0, 0.0).astype(bf16)
+            pick = jnp.where(ids == fold[...].reshape(1, LON), 1.0, 0.0).astype(bf16)
             srcc[rows, :] = pick
             return 0
 
@@ -172,7 +186,7 @@
         inc_a[r] = jnp.where(ids == celln[r:r + 1, :], cellw[r:r + 1, :], 0.0).astype(bf16)
 
     ready("sendr", "esrc", "etgt")
-    send_t = sendr[...].astype(f32).T
+    send_t = sendr[...].astype(f32)
     lane256 = lax.broadcasted_iota(i32, (CAP, 256), 1).astype(f32)
     for p in range(SPACE):
         sel_o[p * CAP:(p + 1) * CAP, :] = jnp.where(send_t[:, p:p + 1] == lane256, 1.0, 0.0).astype(bf16)
@@ -203,7 +217,7 @@
         row = ridx[which, pl.ds(e, 1), :].astype(f32)
         return jnp.broadcast_to(row, (128, 128)).T
 
-    def build(e, _):
+    def build_one(e):
         rows = pl.ds(pl.multiple_of(e * 128, 128), 128)
         c = column(0, e)
         hb = jnp.where(c >= 2048.0, 1.0, 0.0)
@@ -215,8 +229,8 @@
         one = jnp.ones((128, 128), bf16)
         zero = jnp.zeros((128, 128), bf16)
         for tile in range(10):
-            at = tile if tile < 2 else tile + 2
-            onehot[rows, at * 128:(at + 1) * 128] = jnp.where(m == jnp.asarray(tile, bf16), one, zero)
+            to = tile if tile < 2 else tile + 2
+            onehot[rows, to * 128:(to + 1) * 128] = jnp.where(m == jnp.asarray(tile, bf16), one, zero)
         c = column(1, e)
         for tile in range(2):
             onehot[rows, (2 + tile) * 128:(3 + tile) * 128] = jnp.where(
@@ -224,9 +238,14 @@
             ).astype(bf16)
         ids = lax.broadcasted_iota(i32, (NODES, 128), 0)
         pool_p[:, rows] = jnp.where(ids == ridx[2, pl.ds(e, 1), :], 1.0, 0.0).astype(bf16)
+
+    def build(b, _):
+        for k in range(UNROLL):
+            build_one(b * UNROLL + k)
         return 0
 
-    FIRST = 20
+    BUILDS = EDGES // 128 // UNROLL
+    FIRST = BUILDS // 2
     lax.fori_loop(0, FIRST, build, 0)
 
     halo[0].wait_recv()
@@ -259,7 +278,7 @@
     nodes4[ch] = mine
     g_nodes = gather_start(nodes4, 0)
     ready("srcw", "tgtw")
-    lax.fori_loop(FIRST, FIRST + 4, build, 0)
+    lax.fori_loop(FIRST, BUILDS, build, 0)
     for c in g_nodes:
         c.wait_recv()
     nodes = gathered(nodes4)
@@ -271,31 +290,38 @@
         outg[b * 8:(b + 1) * 8] = picked.reshape(8, CAP, COLS)
 
     def a2a_copy(pos, j):
-        peer = ((my + j // 4) % NY) * 32 + ((mz + SHIFTS[pos]) % NZ) * 4 + (mx + j % 4) % NX
+        peer = at(j // 4, SHIFTS[pos], j % 4)
         sl = pos * 8 + j
         return pltpu.make_async_remote_copy(
-            src_ref=outg.at[peer], dst_ref=incoming.at[sl], send_sem=a2a_send.at[sl], recv_sem=a2a_recv.at[sl],
+            src_ref=outg.at[peer], dst_ref=incoming.at[sl], send_sem=a2a_send.at[0], recv_sem=a2a_recv.at[pos // 2],
             device_id={"space": peer}, device_id_type=MESH,
         )
 
-    for pos in range(8):
+    def slots(first, count, group):
+        part = incoming.at[pl.ds(first, count)]
+        return pltpu.make_async_remote_copy(
+            src_ref=outg.at[pl.ds(first, count)], dst_ref=part, send_sem=a2a_send.at[0], recv_sem=a2a_recv.at[group],
+            device_id={"space": (me + 1) % SPACE}, device_id_type=MESH,
+        )
+
+    pl.semaphore_wait(near_sem.at[1], 1)
+    for pos in (1, 0, 2, 3, 4, 5, 6, 7):
         def go(j, _, pos=pos):
             a2a_copy(pos, j).start()
             return 0
         lax.fori_loop(1 if SHIFTS[pos] == 0 else 0, 8, go, 0)
-    incoming[8] = outg[me]
+    incoming[0] = outg[me]
 
     table[256:256 + NODES, :] = dot(nodes, tgtw[...]).astype(bf16)
-    lax.fori_loop(FIRST + 4, EDGES // 128, build, 0)
     ready("edgew", "edgeb", "e0", "e1")
     ebias = edgeb[...].astype(f32)
 
     def own(e, _):
-        rows = pl.ds(pl.multiple_of(e * 256, 256), 256)
+        rows = pl.ds(pl.multiple_of(e * ECH, ECH), ECH)
         acc1[rows, :] = dot(edge[rows, :], edgew[...]) + dot(onehot[rows, 0:512], table[...]) + ebias
         return 0
 
-    lax.fori_loop(0, EDGES // 256, own, 0)
+    lax.fori_loop(0, EDGES // ECH, own, 0)
 
     ready("selfw", "nodeb", "readn", "readw", "msgw", "inw", "outw", "gain")
     self_part = dot(nodes, selfw[...]) + nodeb[...].astype(f32)
@@ -308,6 +334,8 @@
         rwt[:, LON:LONP] = jnp.zeros((NODES, LONP - LON), f32)
         for tile in range(LONP // 128):
             rmat[r, tile * 128:(tile + 1) * 128, :] = rwt[:, tile * 128:(tile + 1) * 128].T.astype(bf16)
+    rmat_copy = pltpu.make_async_copy(rmat, rmat_h, rmat_sem.at[0])
+    rmat_copy.start()
 
     def group_table(g):
         left = incoming[16 * g:16 * g + 8].reshape(256, COLS)
@@ -315,33 +343,30 @@
         return jnp.concatenate([left, right], axis=1)
 
     def arrive(g):
-        for pos in (2 * g, 2 * g + 1):
-            def got(j, _, pos=pos):
-                a2a_copy(pos, j).wait_recv()
-                return 0
-            lax.fori_loop(1 if SHIFTS[pos] == 0 else 0, 8, got, 0)
+        first = 1 if g == 0 else 0
+        slots(16 * g + first, 16 - first, g).wait_recv()
 
     for g in range(3):
         arrive(g)
         tg = group_table(g)
 
         def remote_part(e, _, g=g, tg=tg):
-            rows = pl.ds(pl.multiple_of(e * 256, 256), 256)
+            rows = pl.ds(pl.multiple_of(e * ECH, ECH), ECH)
             d = dot(onehot[rows, 512 + 256 * g:768 + 256 * g], tg)
             acc2[rows, :] = d if g == 0 else acc2[rows, :] + d
             return 0
 
-        lax.fori_loop(0, EDGES // 256, remote_part, 0)
+        lax.fori_loop(0, EDGES // ECH, remote_part, 0)
     arrive(3)
     tg = group_table(3)
 
     def finish(e, pooled):
-        rows = pl.ds(pl.multiple_of(e * 256, 256), 256)
+        rows = pl.ds(pl.multiple_of(e * ECH, ECH), ECH)
         d = dot(onehot[rows, 1280:1536], tg) + acc2[rows, :]
         pre = acc1[rows, :] + jnp.where(half_b[rows, :].astype(f32) > 0.5, d[:, COLS:], d[:, :COLS])
         return pooled + dot(pool_p[:, rows], silu(pre).astype(bf16))
 
-    pooled = lax.fori_loop(0, EDGES // 256, finish, jnp.zeros((NODES, COLS), f32))
+    pooled = lax.fori_loop(0, EDGES // ECH, finish, jnp.zeros((NODES, COLS), f32))
     pool4[ch] = pooled.astype(bf16)
     g_pool = gather_start(pool4, 1)
     for c in g_pool:
@@ -359,21 +384,35 @@
     own_cols = pl.ds(pl.multiple_of(ch * COLS, COLS), COLS)
     result = (mine.astype(f32) + upd[:, own_cols]).astype(bf16)
     node_out[...] = result
-    for r in range(BAND):
-        for m in chunks:
-            rows = pl.ds(m * MCH, MCH)
-            got = dot(rmat[r, rows, :], result)
-            grid_out[r, rows, :] = (x[r, rows, own_cols].astype(f32) + got).astype(bf16)
 
     halo[0].wait_send()
     halo[1].wait_send()
     for c in g_nodes + g_pool + g_hid:
         c.wait_send()
-    for pos in range(8):
-        def left(j, _, pos=pos):
-            a2a_copy(pos, j).wait_send()
-            return 0
-        lax.fori_loop(1 if SHIFTS[pos] == 0 else 0, 8, left, 0)
+    slots(0, SPACE - 1, 0).wait_send()
+    rmat_copy.wait()
+
+
+def read_back(grid_h, rmat, node_h, node_o, grid_o, x, out, sem):
+    ch = lax.axis_index("chan")
+    own_cols = pl.ds(pl.multiple_of(ch * COLS, COLS), COLS)
+    bands = [pltpu.make_async_copy(grid_h.at[r, :, own_cols], x.at[r], sem.at[r]) for r in range(BAND)]
+    for c in bands:
+        c.start()
+    node_copy = pltpu.make_async_copy(node_h, node_o, sem.at[6])
+    node_copy.start()
+    result = node_h[...]
+    done = []
+    for r in range(BAND):
+        bands[r].wait()
+        for m in range(LON // MCH):
+            rows = pl.ds(m * MCH, MCH)
+            out[r, rows, :] = (x[r, rows, :].astype(f32) + dot(rmat[r, rows, :], result)).astype(bf16)
+        c = pltpu.make_async_copy(out.at[r], grid_o.at[r], sem.at[3 + r])
+        c.start()
+        done.append(c)
+    for c in done + [node_copy]:
+        c.wait()
 
 
 def shards(*args):
@@ -385,21 +424,21 @@
     V = pltpu.VMEM
     in_specs = [anyspace] * 24
     in_specs[20] = pl.BlockSpec(memory_space=pltpu.SMEM)
-    return pl.pallas_call(
+    result, rmat = pl.pallas_call(
         kernel,
         out_shape=(
             jax.ShapeDtypeStruct((NODES, COLS), bf16),
-            jax.ShapeDtypeStruct((BAND, LON, COLS), bf16),
+            jax.ShapeDtypeStruct((BAND, LONP, NODES), bf16),
         ),
         in_specs=in_specs,
-        out_specs=(vmem, vmem),
+        out_specs=(vmem, anyspace),
         scratch_shapes=[
-            V((BAND, LON, FEAT), bf16), V((1, LON), i32), V((NODES, COLS), bf16), V((EDGES, FEAT), bf16),
+            V((BAND, LON, FEAT), bf16), V((LON,), i32), V((NODES, COLS), bf16), V((EDGES, FEAT), bf16),
             V((3, FEAT, 3 * COLS), bf16), V((1, COLS), bf16), V((FEAT, COLS), bf16), V((FEAT, COLS), bf16),
             V((FEAT, COLS), bf16), V((1, COLS), bf16),
             V((FEAT, FEAT), bf16), V((FEAT, COLS), bf16), V((FEAT, COLS), bf16), V((1, COLS), bf16),
             V((FEAT, FEAT), bf16), V((1, FEAT), f32), V((BAND, LON), i32), V((BAND, LON), f32),
-            V((40, 128), i32), V((40, 128), i32), V((SPACE, CAP), i32), V((3, BAND, LON), i32), V((3, BAND, LON), f32),
+            V((40, 128), i32), V((40, 128), i32), V((CAP, SPACE), i32), V((3, BAND, LON), i32), V((3, BAND, LON), f32),
             V((LON + 16, 3 * COLS), f32), V((2, LON, COLS), f32), V((2, LON, COLS), bf16), V((2, LON, COLS), bf16),
             V((BAND, LON, COLS), bf16), V((BAND, NODES, LON), bf16), V((SPACE * CAP, 256), bf16),
             V((SPACE, CAP, COLS), bf16), V((512, COLS), bf16),
@@ -410,17 +449,28 @@
             V((LON, LON), bf16),
             pltpu.SemaphoreType.DMA((40,)), pltpu.SemaphoreType.DMA((2,)), pltpu.SemaphoreType.DMA((2,)),
             pltpu.SemaphoreType.DMA((3, CHAN)), pltpu.SemaphoreType.DMA((3, CHAN)),
-            pltpu.SemaphoreType.DMA((SPACE,)), pltpu.SemaphoreType.DMA((SPACE,)),
+            pltpu.SemaphoreType.DMA((1,)), pltpu.SemaphoreType.DMA((4,)), pltpu.SemaphoreType.DMA((1,)),
+            pltpu.SemaphoreType.REGULAR((2,)),
         ],
         compiler_params=pltpu.CompilerParams(
             collective_id=0, has_side_effects=True, vmem_limit_bytes=60 * 1024 * 1024
         ),
     )(
-        grid_state, fold_columns.reshape(1, LON), mesh_state, edge_state, conv_weight, conv_bias.reshape(1, COLS),
+        grid_state, fold_columns, mesh_state, edge_state, conv_weight, conv_bias.reshape(1, COLS),
         source_weight, target_weight, edge_weight, edge_bias.reshape(1, COLS), message_weight, self_weight,
         inbox_weight, node_bias.reshape(1, COLS), output_weight, output_gain.reshape(1, FEAT), cell_node, cell_weight,
-        edge_source.reshape(40, 128), edge_target.reshape(40, 128), edge_count, send_rows, read_node, read_weight,
+        edge_source.reshape(40, 128), edge_target.reshape(40, 128), edge_count, send_rows.transpose(0, 2, 1), read_node, read_weight,
     )
+    return pl.pallas_call(
+        read_back,
+        out_shape=(
+            jax.ShapeDtypeStruct((NODES, COLS), bf16),
+            jax.ShapeDtypeStruct((BAND, LON, COLS), bf16),
+        ),
+        in_specs=[anyspace, vmem, vmem],
+        out_specs=(anyspace, anyspace),
+        scratch_shapes=[V((BAND, LON, COLS), bf16), V((BAND, LON, COLS), bf16), pltpu.SemaphoreType.DMA((7,))],
+    )(grid_state, rmat, result)
 
 
 def solution(mesh):

time: 74.5 us -> 56.1 us (0.75)
  Pallas kernels: 66.9 us -> 54.7 us
  local copies, waits for them, and re-layouts: 5.97 us -> 0 us
    pallas_call x1, Pallas kernels: 66.9 us -> 50.9 us  [shards(): pl.pallas_call(kernel, out_shape=(jax.ShapeDtypeStruct((NODES, COLS), bf1...]
    unnamed x3 -> x0, local copies, waits for them, and re-layouts: 4.7 us -> none
    pallas_call x0 -> x1, Pallas kernels: none -> 3.75 us  [shards(): pl.pallas_call(read_back, out_shape=(jax.ShapeDtypeStruct((NODES, COLS),...]
    reshape x1 -> x0, local copies, waits for them, and re-layouts: 1.27 us -> none  [shards(): fold_columns.reshape(1, LON)]
where the time goes in v2:
time: 56.1 us; the launch traced here: 56 us
  Pallas kernels  54.7 us (98%)
  between operations  1.29 us (2%)
    pallas_call x1, Pallas kernels, shards(): pl.pallas_call(kernel, out_shape=(jax.ShapeDtypeStruct((NODES, COLS), bf1...  50.9 us
    pallas_call x1, Pallas kernels, shards(): pl.pallas_call(read_back, out_shape=(jax.ShapeDtypeStruct((NODES, COLS),...  3.75 us

profile of v2, /device:TPU:1, one launch (start us, length us, event | category | flops | bytes accessed | tf_op | source)
XLA Modules:
  0.0 56.0 jit_solution(16199002355437807491)
XLA Ops:
  1.3 50.9 %shard_map.239 = (bf16[160,128]{1,0:T(8,128)(2,1)}, bf16[3,768,160]{2,1,0:T(8,128)(2,1)}) custom-call(bf16[3,720,512]{2,1,0:T(8,128)(2,1)} %grid_h.3, s32[720]{0:T(1024)} %fold_h.1, bf16[160,128]{1,0:T(8,128)(2,1)} %mesh_h.1, bf16[5120,512]{1,0:T(8,128)(2,1)} %edge_h.1, bf16[3,3,512,128]{3,2,1,0:T(8,128)(2,1)} %convw_h.1, bf16[1,128]{1,0:T(2,128)(2,1)} %bitcast.11, ...), custom_call_target="tpu_custom_call" | custom-call | tf_op jit(solution)/shard_map/pallas_call | solution.py:427
  52.2 3.8 %shard_map.240 = (bf16[160,128]{1,0:T(8,128)(2,1)}, bf16[3,720,128]{2,1,0:T(8,128)(2,1)}) custom-call(bf16[3,720,512]{2,1,0:T(8,128)(2,1)} %grid_h.3, bf16[3,768,160]{2,1,0:T(8,128)(2,1)} %get-tuple-element.4.rmat, bf16[160,128]{1,0:T(8,128)(2,1)} %get-tuple-element.5.node_h), custom_call_target="tpu_custom_call" | custom-call | tf_op jit(solution)/shard_map/pallas_call | solution.py:464

commit v3 on v2

--- a/solution.py
+++ b/solution.py
@@ -23,6 +23,7 @@
 SHIFTS = (0, 4, 3, 5, 2, 6, 1, 7)
 ECH = 1280
 UNROLL = 4
+EARLY = 4
 
 
 def dot(a, b):
@@ -66,14 +67,22 @@
 
     load("x0", grid_h.at[0], x.at[0])
     load_w(2)
+    load("x2", grid_h.at[2], x.at[2])
+    load_w(0)
+    load("x1", grid_h.at[1], x.at[1])
+    load_w(1)
 
     barrier = pltpu.get_barrier_semaphore()
 
     def hail(sem, **where):
         pl.semaphore_signal(sem, inc=1, device_id=where, device_id_type=MESH)
 
+    y_at = [((my + d) % NY) * 32 for d in range(NY)]
+    z_at = [((mz + d) % NZ) * 4 for d in range(NZ)]
+    x_at = [(mx + d) % NX for d in range(NX)]
+
     def at(dy, dz, dx):
-        return ((my + dy) % NY) * 32 + ((mz + dz) % NZ) * 4 + (mx + dx) % NX
+        return y_at[dy] + z_at[dz] + x_at[dx]
 
     hail(barrier, space=(me + 1) % SPACE)
     hail(barrier, space=(me + SPACE - 1) % SPACE)
@@ -84,18 +93,9 @@
         hail(barrier, space=at(0, 0, d))
     for d in range(1, NZ):
         hail(barrier, space=at(0, d, 0))
-    load("x2", grid_h.at[2], x.at[2])
-    load_w(0)
-    load("x1", grid_h.at[1], x.at[1])
-    load_w(1)
     for name, s, d in (
         ("convb", convb_h, convb), ("celln", celln_h, celln), ("cellw", cellw_h, cellw),
-        ("sendr", send_h.at[0], sendr), ("esrc", esrc_h, esrc), ("etgt", etgt_h, etgt),
-        ("fold", fold_h, fold), ("mesh", mesh_h, mesh_v), ("srcw", srcw_h, srcw), ("tgtw", tgtw_h, tgtw),
-        ("edgew", edgew_h, edgew), ("edgeb", edgeb_h, edgeb),
-        ("e0", edge_h.at[0:2560], edge.at[0:2560]), ("e1", edge_h.at[2560:5120], edge.at[2560:5120]),
-        ("selfw", selfw_h, selfw), ("msgw", msgw_h, msgw), ("inw", inw_h, inw), ("nodeb", nodeb_h, nodeb),
-        ("outw", outw_h, outw), ("gain", gain_h, gain), ("readn", readn_h, readn), ("readw", readw_h, readw),
+        ("sendr", send_h.at[0], sendr), ("fold", fold_h, fold), ("mesh", mesh_h, mesh_v), ("srcw", srcw_h, srcw),
     ):
         load(name, s, d)
 
@@ -146,6 +146,14 @@
     hail(near_sem.at[1], space=at(1, 0, 0))
 
     ready("x1", ("w", 1, 0), ("w", 1, 1), ("w", 1, 2), "convb", "celln", "cellw")
+    for name, s, d in (
+        ("esrc", esrc_h, esrc), ("etgt", etgt_h, etgt), ("tgtw", tgtw_h, tgtw),
+        ("edgew", edgew_h, edgew), ("edgeb", edgeb_h, edgeb),
+        ("e0", edge_h.at[0:2560], edge.at[0:2560]), ("e1", edge_h.at[2560:5120], edge.at[2560:5120]),
+        ("selfw", selfw_h, selfw), ("msgw", msgw_h, msgw), ("inw", inw_h, inw), ("nodeb", nodeb_h, nodeb),
+        ("outw", outw_h, outw), ("gain", gain_h, gain), ("readn", readn_h, readn), ("readw", readw_h, readw),
+    ):
+        load(name, s, d)
     bias = convb[...].astype(f32)
     for r, terms in (
         (0, [(x.at[0], 1), (x.at[1], 2)]),
@@ -185,12 +193,45 @@
         ids = lax.broadcasted_iota(i32, (NODES, LON), 0)
         inc_a[r] = jnp.where(ids == celln[r:r + 1, :], cellw[r:r + 1, :], 0.0).astype(bf16)
 
-    ready("sendr", "esrc", "etgt")
+    ready("sendr")
     send_t = sendr[...].astype(f32)
     lane256 = lax.broadcasted_iota(i32, (CAP, 256), 1).astype(f32)
     for p in range(SPACE):
         sel_o[p * CAP:(p + 1) * CAP, :] = jnp.where(send_t[:, p:p + 1] == lane256, 1.0, 0.0).astype(bf16)
 
+    halo[0].wait_recv()
+    halo[1].wait_recv()
+    south_ok = jnp.where(me > 0, 1.0, 0.0)
+    north_ok = jnp.where(me < SPACE - 1, 1.0, 0.0)
+    for m in chunks:
+        rows = pl.ds(m * MCH, MCH)
+        act[0, rows, :] = silu(cpart[0, rows, :] + halo_in[1, rows, :].astype(f32) * south_ok).astype(bf16)
+        act[2, rows, :] = silu(cpart[1, rows, :] + halo_in[0, rows, :].astype(f32) * north_ok).astype(bf16)
+    ready("mesh")
+    agg = dot(inc_a[0], act[0]) + dot(inc_a[1], act[1]) + dot(inc_a[2], act[2])
+    mine = (mesh_v[...].astype(f32) + agg).astype(bf16)
+
+    def gather_start(buf, stage):
+        out = []
+        for d in range(1, CHAN):
+            c = pltpu.make_async_remote_copy(
+                src_ref=buf.at[ch], dst_ref=buf.at[ch],
+                send_sem=gat_send.at[stage, d], recv_sem=gat_recv.at[stage, d],
+                device_id={"chan": (ch + d) % CHAN}, device_id_type=MESH,
+            )
+            c.start()
+            out.append(c)
+        return out
+
+    def gathered(buf):
+        return jnp.concatenate([buf[0], buf[1], buf[2], buf[3]], axis=1)
+
+    nodes4[ch] = mine
+    g_nodes = gather_start(nodes4, 0)
+    ready("srcw", "tgtw")
+    table[...] = jnp.zeros_like(table)
+
+    ready("esrc", "etgt")
     s = esrc[...]
     u = s - NODES
     q = lax.shift_right_logical(u, 5) & 63
@@ -245,52 +286,18 @@
         return 0
 
     BUILDS = EDGES // 128 // UNROLL
-    FIRST = BUILDS // 2
-    lax.fori_loop(0, FIRST, build, 0)
-
-    halo[0].wait_recv()
-    halo[1].wait_recv()
-    south_ok = jnp.where(me > 0, 1.0, 0.0)
-    north_ok = jnp.where(me < SPACE - 1, 1.0, 0.0)
-    for m in chunks:
-        rows = pl.ds(m * MCH, MCH)
-        act[0, rows, :] = silu(cpart[0, rows, :] + halo_in[1, rows, :].astype(f32) * south_ok).astype(bf16)
-        act[2, rows, :] = silu(cpart[1, rows, :] + halo_in[0, rows, :].astype(f32) * north_ok).astype(bf16)
-    ready("mesh")
-    agg = dot(inc_a[0], act[0]) + dot(inc_a[1], act[1]) + dot(inc_a[2], act[2])
-    mine = (mesh_v[...].astype(f32) + agg).astype(bf16)
-
-    def gather_start(buf, stage):
-        out = []
-        for d in range(1, CHAN):
-            c = pltpu.make_async_remote_copy(
-                src_ref=buf.at[ch], dst_ref=buf.at[ch],
-                send_sem=gat_send.at[stage, d], recv_sem=gat_recv.at[stage, d],
-                device_id={"chan": (ch + d) % CHAN}, device_id_type=MESH,
-            )
-            c.start()
-            out.append(c)
-        return out
-
-    def gathered(buf):
-        return jnp.concatenate([buf[0], buf[1], buf[2], buf[3]], axis=1)
-
-    nodes4[ch] = mine
-    g_nodes = gather_start(nodes4, 0)
-    ready("srcw", "tgtw")
-    lax.fori_loop(FIRST, BUILDS, build, 0)
+    lax.fori_loop(0, EARLY, build, 0)
     for c in g_nodes:
         c.wait_recv()
     nodes = gathered(nodes4)
     sent = dot(nodes, srcw[...]).astype(bf16)
-    table[...] = jnp.zeros_like(table)
     table[0:NODES, :] = sent
     for b in range(SPACE * CAP // 256):
         picked = dot(sel_o[b * 256:(b + 1) * 256, :], table[0:256, :]).astype(bf16)
         outg[b * 8:(b + 1) * 8] = picked.reshape(8, CAP, COLS)
 
     def a2a_copy(pos, j):
-        peer = at(j // 4, SHIFTS[pos], j % 4)
+        peer = y_at[j // 4] + z_at[SHIFTS[pos]] + x_at[j % 4]
         sl = pos * 8 + j
         return pltpu.make_async_remote_copy(
             src_ref=outg.at[peer], dst_ref=incoming.at[sl], send_sem=a2a_send.at[0], recv_sem=a2a_recv.at[pos // 2],
@@ -306,13 +313,13 @@
 
     pl.semaphore_wait(near_sem.at[1], 1)
     for pos in (1, 0, 2, 3, 4, 5, 6, 7):
-        def go(j, _, pos=pos):
-            a2a_copy(pos, j).start()
-            return 0
-        lax.fori_loop(1 if SHIFTS[pos] == 0 else 0, 8, go, 0)
+        for j in range(8):
+            if SHIFTS[pos] or j:
+                a2a_copy(pos, j).start()
     incoming[0] = outg[me]
 
     table[256:256 + NODES, :] = dot(nodes, tgtw[...]).astype(bf16)
+    lax.fori_loop(EARLY, BUILDS, build, 0)
     ready("edgew", "edgeb", "e0", "e1")
     ebias = edgeb[...].astype(f32)
 
@@ -353,7 +360,11 @@
         def remote_part(e, _, g=g, tg=tg):
             rows = pl.ds(pl.multiple_of(e * ECH, ECH), ECH)
             d = dot(onehot[rows, 512 + 256 * g:768 + 256 * g], tg)
-            acc2[rows, :] = d if g == 0 else acc2[rows, :] + d
+            if g == 0:
+                base = acc1[rows, :]
+                acc2[rows, :] = d + jnp.concatenate([base, base], axis=1)
+            else:
+                acc2[rows, :] = acc2[rows, :] + d
             return 0
 
         lax.fori_loop(0, EDGES // ECH, remote_part, 0)
@@ -363,7 +374,7 @@
     def finish(e, pooled):
         rows = pl.ds(pl.multiple_of(e * ECH, ECH), ECH)
         d = dot(onehot[rows, 1280:1536], tg) + acc2[rows, :]
-        pre = acc1[rows, :] + jnp.where(half_b[rows, :].astype(f32) > 0.5, d[:, COLS:], d[:, :COLS])
+        pre = jnp.where(half_b[rows, :].astype(f32) > 0.5, d[:, COLS:], d[:, :COLS])
         return pooled + dot(pool_p[:, rows], silu(pre).astype(bf16))
 
     pooled = lax.fori_loop(0, EDGES // ECH, finish, jnp.zeros((NODES, COLS), f32))
@@ -393,25 +404,33 @@
     rmat_copy.wait()
 
 
-def read_back(grid_h, rmat, node_h, node_o, grid_o, x, out, sem):
+def read_back(grid_h, rmat_h, node_h, node_o, grid_o, x, rmat, node, out, sem):
     ch = lax.axis_index("chan")
     own_cols = pl.ds(pl.multiple_of(ch * COLS, COLS), COLS)
-    bands = [pltpu.make_async_copy(grid_h.at[r, :, own_cols], x.at[r], sem.at[r]) for r in range(BAND)]
-    for c in bands:
-        c.start()
-    node_copy = pltpu.make_async_copy(node_h, node_o, sem.at[6])
-    node_copy.start()
-    result = node_h[...]
-    done = []
+    node_in = pltpu.make_async_copy(node_h, node, sem.at[6])
+    node_in.start()
+    bands = []
     for r in range(BAND):
-        bands[r].wait()
+        bands.append((
+            pltpu.make_async_copy(grid_h.at[r, :, own_cols], x.at[r], sem.at[r]),
+            pltpu.make_async_copy(rmat_h.at[r, 0:LON], rmat.at[r], sem.at[8 + r]),
+        ))
+        for c in bands[-1]:
+            c.start()
+    done = [pltpu.make_async_copy(node_h, node_o, sem.at[7])]
+    done[0].start()
+    node_in.wait()
+    result = node[...]
+    for r in range(BAND):
+        for c in bands[r]:
+            c.wait()
         for m in range(LON // MCH):
             rows = pl.ds(m * MCH, MCH)
             out[r, rows, :] = (x[r, rows, :].astype(f32) + dot(rmat[r, rows, :], result)).astype(bf16)
         c = pltpu.make_async_copy(out.at[r], grid_o.at[r], sem.at[3 + r])
         c.start()
         done.append(c)
-    for c in done + [node_copy]:
+    for c in done:
         c.wait()
 
 
@@ -467,9 +486,12 @@
             jax.ShapeDtypeStruct((NODES, COLS), bf16),
             jax.ShapeDtypeStruct((BAND, LON, COLS), bf16),
         ),
-        in_specs=[anyspace, vmem, vmem],
+        in_specs=[anyspace, anyspace, anyspace],
         out_specs=(anyspace, anyspace),
-        scratch_shapes=[V((BAND, LON, COLS), bf16), V((BAND, LON, COLS), bf16), pltpu.SemaphoreType.DMA((7,))],
+        scratch_shapes=[
+            V((BAND, LON, COLS), bf16), V((BAND, LON, NODES), bf16), V((NODES, COLS), bf16),
+            V((BAND, LON, COLS), bf16), pltpu.SemaphoreType.DMA((11,)),
+        ],
     )(grid_state, rmat, result)
 
 

time: 56.1 us -> 53.6 us (0.955)
  Pallas kernels: 54.7 us -> 52 us
    pallas_call x1, Pallas kernels: 50.9 us -> 49.3 us  [shards(): pl.pallas_call(kernel, out_shape=(jax.ShapeDtypeStruct((NODES, COLS), bf1...]
    pallas_call x1, Pallas kernels: 3.75 us -> 2.69 us  [shards(): pl.pallas_call(read_back, out_shape=(jax.ShapeDtypeStruct((NODES, COLS),...]
where the time goes in v3:
time: 53.6 us; the launch traced here: 53.5 us
  Pallas kernels  52 us (97%)
  between operations  1.45 us (3%)
    pallas_call x1, Pallas kernels, shards(): pl.pallas_call(kernel, out_shape=(jax.ShapeDtypeStruct((NODES, COLS), bf1...  49.3 us
    pallas_call x1, Pallas kernels, shards(): pl.pallas_call(read_back, out_shape=(jax.ShapeDtypeStruct((NODES, COLS),...  2.69 us

profile of v3, /device:TPU:1, one launch (start us, length us, event | category | flops | bytes accessed | tf_op | source)
XLA Modules:
  0.0 53.5 jit_solution(16445811787441788970)
XLA Ops:
  1.3 49.3 %shard_map.239 = (bf16[160,128]{1,0:T(8,128)(2,1)}, bf16[3,768,160]{2,1,0:T(8,128)(2,1)}) custom-call(bf16[3,720,512]{2,1,0:T(8,128)(2,1)} %grid_h.3, s32[720]{0:T(1024)} %fold_h.1, bf16[160,128]{1,0:T(8,128)(2,1)} %mesh_h.1, bf16[5120,512]{1,0:T(8,128)(2,1)} %edge_h.1, bf16[3,3,512,128]{3,2,1,0:T(8,128)(2,1)} %convw_h.1, bf16[1,128]{1,0:T(2,128)(2,1)} %bitcast.11, ...), custom_call_target="tpu_custom_call" | custom-call | tf_op jit(solution)/shard_map/pallas_call | solution.py:446
  50.6 2.7 %shard_map.240 = (bf16[160,128]{1,0:T(8,128)(2,1)}, bf16[3,720,128]{2,1,0:T(8,128)(2,1)}) custom-call(bf16[3,720,512]{2,1,0:T(8,128)(2,1)} %grid_h.3, bf16[3,768,160]{2,1,0:T(8,128)(2,1)} %get-tuple-element.4.rmat_h, bf16[160,128]{1,0:T(8,128)(2,1)} %get-tuple-element.5.node_h), custom_call_target="tpu_custom_call" | custom-call | tf_op jit(solution)/shard_map/pallas_call | solution.py:483

commit v4 on v3

--- a/solution.py
+++ b/solution.py
@@ -40,8 +40,8 @@
     ecount, send_h, readn_h, readw_h,
     node_out, rmat_h,
     x, fold, mesh_v, edge, wcat, convb, srcw, tgtw, edgew, edgeb,
-    msgw, selfw, inw, nodeb, outw, gain, celln, cellw, esrc, etgt, sendr, readn, readw,
-    z, cpart, halo_out, halo_in, act, inc_a, sel_o, outg, table, nodes4, pool4, hid4,
+    msgw, selfw, nodeb, outw, gain, celln, cellw, esrc, etgt, sendr, readn, readw,
+    z, cpart, halo_out, halo_in, act, inc_a, sel_o, outg, table, nodes4, pool4, self4, inw4, both,
     onehot, half_b, pool_p, acc1, acc2, incoming, ridx, rwt, rmat, upd, srcc,
     load_sem, halo_send, halo_recv, gat_send, gat_recv, a2a_send, a2a_recv, rmat_sem, near_sem,
 ):
@@ -95,9 +95,27 @@
         hail(barrier, space=at(0, d, 0))
     for name, s, d in (
         ("convb", convb_h, convb), ("celln", celln_h, celln), ("cellw", cellw_h, cellw),
+        ("inw", inw_h, inw4.at[ch]),
         ("sendr", send_h.at[0], sendr), ("fold", fold_h, fold), ("mesh", mesh_h, mesh_v), ("srcw", srcw_h, srcw),
     ):
         load(name, s, d)
+
+    sibling = ch + 1 - 2 * (ch % 2)
+    group = ((ch + 2) % CHAN, (sibling + 2) % CHAN, sibling)
+
+    def gather_start(buf, stage):
+        out = []
+        for k, peer in enumerate(group):
+            c = pltpu.make_async_remote_copy(
+                src_ref=buf.at[ch], dst_ref=buf.at[ch], send_sem=gat_send.at[stage, k], recv_sem=gat_recv.at[stage, k],
+                device_id={"chan": peer}, device_id_type=MESH,
+            )
+            c.start()
+            out.append(c)
+        return out
+
+    def gathered(buf):
+        return jnp.concatenate([buf[c] for c in range(CHAN)], axis=1)
 
     def conv_z(terms):
         for m in range(LON // MCH):
@@ -142,6 +160,8 @@
     for m in chunks:
         halo_out[1, pl.ds(m * MCH, MCH), :] = shifted(m).astype(bf16)
     halo[1].start()
+    ready("inw")
+    g_inw = gather_start(inw4, 1)
     pl.semaphore_wait(near_sem.at[0], NX - 1)
     hail(near_sem.at[1], space=at(1, 0, 0))
 
@@ -150,7 +170,7 @@
         ("esrc", esrc_h, esrc), ("etgt", etgt_h, etgt), ("tgtw", tgtw_h, tgtw),
         ("edgew", edgew_h, edgew), ("edgeb", edgeb_h, edgeb),
         ("e0", edge_h.at[0:2560], edge.at[0:2560]), ("e1", edge_h.at[2560:5120], edge.at[2560:5120]),
-        ("selfw", selfw_h, selfw), ("msgw", msgw_h, msgw), ("inw", inw_h, inw), ("nodeb", nodeb_h, nodeb),
+        ("selfw", selfw_h, selfw), ("msgw", msgw_h, msgw), ("nodeb", nodeb_h, nodeb),
         ("outw", outw_h, outw), ("gain", gain_h, gain), ("readn", readn_h, readn), ("readw", readw_h, readw),
     ):
         load(name, s, d)
@@ -210,21 +230,6 @@
     ready("mesh")
     agg = dot(inc_a[0], act[0]) + dot(inc_a[1], act[1]) + dot(inc_a[2], act[2])
     mine = (mesh_v[...].astype(f32) + agg).astype(bf16)
-
-    def gather_start(buf, stage):
-        out = []
-        for d in range(1, CHAN):
-            c = pltpu.make_async_remote_copy(
-                src_ref=buf.at[ch], dst_ref=buf.at[ch],
-                send_sem=gat_send.at[stage, d], recv_sem=gat_recv.at[stage, d],
-                device_id={"chan": (ch + d) % CHAN}, device_id_type=MESH,
-            )
-            c.start()
-            out.append(c)
-        return out
-
-    def gathered(buf):
-        return jnp.concatenate([buf[0], buf[1], buf[2], buf[3]], axis=1)
 
     nodes4[ch] = mine
     g_nodes = gather_start(nodes4, 0)
@@ -318,6 +323,9 @@
                 a2a_copy(pos, j).start()
     incoming[0] = outg[me]
 
+    ready("selfw", "nodeb")
+    self4[ch] = (dot(nodes, selfw[...]) + nodeb[...].astype(f32)).astype(bf16)
+    g_self = gather_start(self4, 2)
     table[256:256 + NODES, :] = dot(nodes, tgtw[...]).astype(bf16)
     lax.fori_loop(EARLY, BUILDS, build, 0)
     ready("edgew", "edgeb", "e0", "e1")
@@ -330,8 +338,10 @@
 
     lax.fori_loop(0, EDGES // ECH, own, 0)
 
-    ready("selfw", "nodeb", "readn", "readw", "msgw", "inw", "outw", "gain")
-    self_part = dot(nodes, selfw[...]) + nodeb[...].astype(f32)
+    ready("readn", "readw", "msgw", "outw", "gain")
+    for c in g_inw + g_self:
+        c.wait_recv()
+    both[...] = dot(msgw[...], gathered(inw4)).astype(bf16)
     ids = lax.broadcasted_iota(i32, (NODES, LON), 0)
     for r in range(BAND):
         w = jnp.zeros((NODES, LON), f32)
@@ -379,15 +389,11 @@
 
     pooled = lax.fori_loop(0, EDGES // ECH, finish, jnp.zeros((NODES, COLS), f32))
     pool4[ch] = pooled.astype(bf16)
-    g_pool = gather_start(pool4, 1)
+    g_pool = gather_start(pool4, 3)
     for c in g_pool:
         c.wait_recv()
-    message = dot(gathered(pool4), msgw[...]).astype(bf16)
-    hid4[ch] = silu(self_part + dot(message, inw[...])).astype(bf16)
-    g_hid = gather_start(hid4, 2)
-    for c in g_hid:
-        c.wait_recv()
-    update = dot(gathered(hid4), outw[...])
+    hidden = silu(gathered(self4).astype(f32) + dot(gathered(pool4), both[...])).astype(bf16)
+    update = dot(hidden, outw[...])
     mean = jnp.mean(update, axis=1, keepdims=True)
     centred = update - mean
     var = jnp.mean(jnp.square(centred), axis=1, keepdims=True)
@@ -398,7 +404,7 @@
 
     halo[0].wait_send()
     halo[1].wait_send()
-    for c in g_nodes + g_pool + g_hid:
+    for c in g_nodes + g_inw + g_self + g_pool:
         c.wait_send()
     slots(0, SPACE - 1, 0).wait_send()
     rmat_copy.wait()
@@ -455,19 +461,20 @@
             V((BAND, LON, FEAT), bf16), V((LON,), i32), V((NODES, COLS), bf16), V((EDGES, FEAT), bf16),
             V((3, FEAT, 3 * COLS), bf16), V((1, COLS), bf16), V((FEAT, COLS), bf16), V((FEAT, COLS), bf16),
             V((FEAT, COLS), bf16), V((1, COLS), bf16),
-            V((FEAT, FEAT), bf16), V((FEAT, COLS), bf16), V((FEAT, COLS), bf16), V((1, COLS), bf16),
+            V((FEAT, FEAT), bf16), V((FEAT, COLS), bf16), V((1, COLS), bf16),
             V((FEAT, FEAT), bf16), V((1, FEAT), f32), V((BAND, LON), i32), V((BAND, LON), f32),
             V((40, 128), i32), V((40, 128), i32), V((CAP, SPACE), i32), V((3, BAND, LON), i32), V((3, BAND, LON), f32),
             V((LON + 16, 3 * COLS), f32), V((2, LON, COLS), f32), V((2, LON, COLS), bf16), V((2, LON, COLS), bf16),
             V((BAND, LON, COLS), bf16), V((BAND, NODES, LON), bf16), V((SPACE * CAP, 256), bf16),
             V((SPACE, CAP, COLS), bf16), V((512, COLS), bf16),
             V((CHAN, NODES, COLS), bf16), V((CHAN, NODES, COLS), bf16), V((CHAN, NODES, COLS), bf16),
+            V((CHAN, FEAT, COLS), bf16), V((FEAT, FEAT), bf16),
             V((EDGES, 1536), bf16), V((EDGES, 128), bf16), V((NODES, EDGES), bf16),
             V((EDGES, COLS), f32), V((EDGES, 2 * COLS), f32), V((SPACE, CAP, COLS), bf16),
             V((3, 40, 128), i32), V((NODES, LONP), f32), V((BAND, LONP, NODES), bf16), V((NODES, FEAT), f32),
             V((LON, LON), bf16),
             pltpu.SemaphoreType.DMA((40,)), pltpu.SemaphoreType.DMA((2,)), pltpu.SemaphoreType.DMA((2,)),
-            pltpu.SemaphoreType.DMA((3, CHAN)), pltpu.SemaphoreType.DMA((3, CHAN)),
+            pltpu.SemaphoreType.DMA((4, 3)), pltpu.SemaphoreType.DMA((4, 3)),
             pltpu.SemaphoreType.DMA((1,)), pltpu.SemaphoreType.DMA((4,)), pltpu.SemaphoreType.DMA((1,)),
             pltpu.SemaphoreType.REGULAR((2,)),
         ],

time: 53.6 us -> 50.7 us (0.946)
  Pallas kernels: 52 us -> 49.2 us
    pallas_call x1, Pallas kernels: 49.3 us -> 46.5 us  [shards(): pl.pallas_call(kernel, out_shape=(jax.ShapeDtypeStruct((NODES, COLS), bf1...]
where the time goes in v4:
time: 50.7 us; the launch traced here: 50.6 us
  Pallas kernels  49.2 us (97%)
  between operations  1.45 us (3%)
    pallas_call x1, Pallas kernels, shards(): pl.pallas_call(kernel, out_shape=(jax.ShapeDtypeStruct((NODES, COLS), bf1...  46.5 us
    pallas_call x1, Pallas kernels, shards(): pl.pallas_call(read_back, out_shape=(jax.ShapeDtypeStruct((NODES, COLS),...  2.69 us

profile of v4, /device:TPU:1, one launch (start us, length us, event | category | flops | bytes accessed | tf_op | source)
XLA Modules:
  0.0 50.6 jit_solution(9006076531443710475)
XLA Ops:
  1.3 46.5 %shard_map.239 = (bf16[160,128]{1,0:T(8,128)(2,1)}, bf16[3,768,160]{2,1,0:T(8,128)(2,1)}) custom-call(bf16[3,720,512]{2,1,0:T(8,128)(2,1)} %grid_h.3, s32[720]{0:T(1024)} %fold_h.1, bf16[160,128]{1,0:T(8,128)(2,1)} %mesh_h.1, bf16[5120,512]{1,0:T(8,128)(2,1)} %edge_h.1, bf16[3,3,512,128]{3,2,1,0:T(8,128)(2,1)} %convw_h.1, bf16[1,128]{1,0:T(2,128)(2,1)} %bitcast.11, ...), custom_call_target="tpu_custom_call" | custom-call | tf_op jit(solution)/shard_map/pallas_call | solution.py:452
  47.8 2.7 %shard_map.240 = (bf16[160,128]{1,0:T(8,128)(2,1)}, bf16[3,720,128]{2,1,0:T(8,128)(2,1)}) custom-call(bf16[3,720,512]{2,1,0:T(8,128)(2,1)} %grid_h.3, bf16[3,768,160]{2,1,0:T(8,128)(2,1)} %get-tuple-element.4.rmat_h, bf16[160,128]{1,0:T(8,128)(2,1)} %get-tuple-element.5.node_h), custom_call_target="tpu_custom_call" | custom-call | tf_op jit(solution)/shard_map/pallas_call | solution.py:490

commit v5 on v4

--- a/solution.py
+++ b/solution.py
@@ -21,9 +21,9 @@
 MCH = 240
 LONP = 768
 SHIFTS = (0, 4, 3, 5, 2, 6, 1, 7)
-ECH = 1280
-UNROLL = 4
-EARLY = 4
+ECH = 2560
+UNROLL = 8
+EARLY = 2
 
 
 def dot(a, b):

time: 50.7 us -> 48.7 us (0.961)
  Pallas kernels: 49.2 us -> 47.1 us
    pallas_call x1, Pallas kernels: 46.5 us -> 44.4 us  [shards(): pl.pallas_call(kernel, out_shape=(jax.ShapeDtypeStruct((NODES, COLS), bf1...]
where the time goes in v5:
time: 48.7 us; the launch traced here: 48.6 us
  Pallas kernels  47.1 us (97%)
  between operations  1.45 us (3%)
    pallas_call x1, Pallas kernels, shards(): pl.pallas_call(kernel, out_shape=(jax.ShapeDtypeStruct((NODES, COLS), bf1...  44.4 us
    pallas_call x1, Pallas kernels, shards(): pl.pallas_call(read_back, out_shape=(jax.ShapeDtypeStruct((NODES, COLS),...  2.69 us

profile of v5, /device:TPU:1, one launch (start us, length us, event | category | flops | bytes accessed | tf_op | source)
XLA Modules:
  0.0 48.6 jit_solution(737436761402385250)
XLA Ops:
  1.3 44.4 %shard_map.239 = (bf16[160,128]{1,0:T(8,128)(2,1)}, bf16[3,768,160]{2,1,0:T(8,128)(2,1)}) custom-call(bf16[3,720,512]{2,1,0:T(8,128)(2,1)} %grid_h.3, s32[720]{0:T(1024)} %fold_h.1, bf16[160,128]{1,0:T(8,128)(2,1)} %mesh_h.1, bf16[5120,512]{1,0:T(8,128)(2,1)} %edge_h.1, bf16[3,3,512,128]{3,2,1,0:T(8,128)(2,1)} %convw_h.1, bf16[1,128]{1,0:T(2,128)(2,1)} %bitcast.11, ...), custom_call_target="tpu_custom_call" | custom-call | tf_op jit(solution)/shard_map/pallas_call | solution.py:452
  45.7 2.7 %shard_map.240 = (bf16[160,128]{1,0:T(8,128)(2,1)}, bf16[3,720,128]{2,1,0:T(8,128)(2,1)}) custom-call(bf16[3,720,512]{2,1,0:T(8,128)(2,1)} %grid_h.3, bf16[3,768,160]{2,1,0:T(8,128)(2,1)} %get-tuple-element.4.rmat_h, bf16[160,128]{1,0:T(8,128)(2,1)} %get-tuple-element.5.node_h), custom_call_target="tpu_custom_call" | custom-call | tf_op jit(solution)/shard_map/pallas_call | solution.py:490

commit v6 on v5

--- a/solution.py
+++ b/solution.py
@@ -22,8 +22,8 @@
 LONP = 768
 SHIFTS = (0, 4, 3, 5, 2, 6, 1, 7)
 ECH = 2560
-UNROLL = 8
-EARLY = 2
+UNROLL = 20
+EARLY = 1
 
 
 def dot(a, b):
@@ -213,12 +213,6 @@
         ids = lax.broadcasted_iota(i32, (NODES, LON), 0)
         inc_a[r] = jnp.where(ids == celln[r:r + 1, :], cellw[r:r + 1, :], 0.0).astype(bf16)
 
-    ready("sendr")
-    send_t = sendr[...].astype(f32)
-    lane256 = lax.broadcasted_iota(i32, (CAP, 256), 1).astype(f32)
-    for p in range(SPACE):
-        sel_o[p * CAP:(p + 1) * CAP, :] = jnp.where(send_t[:, p:p + 1] == lane256, 1.0, 0.0).astype(bf16)
-
     halo[0].wait_recv()
     halo[1].wait_recv()
     south_ok = jnp.where(me > 0, 1.0, 0.0)
@@ -235,6 +229,12 @@
     g_nodes = gather_start(nodes4, 0)
     ready("srcw", "tgtw")
     table[...] = jnp.zeros_like(table)
+
+    ready("sendr")
+    send_t = sendr[...].astype(f32)
+    lane256 = lax.broadcasted_iota(i32, (CAP, 256), 1).astype(f32)
+    for p in range(SPACE):
+        sel_o[p * CAP:(p + 1) * CAP, :] = jnp.where(send_t[:, p:p + 1] == lane256, 1.0, 0.0).astype(bf16)
 
     ready("esrc", "etgt")
     s = esrc[...]

time: 48.7 us -> 48.5 us (level)
  no operation moved by 1% of the time
where the time goes in v6:
time: 48.5 us; the launch traced here: 48.4 us
  Pallas kernels  46.9 us (97%)
  between operations  1.45 us (3%)
    pallas_call x1, Pallas kernels, shards(): pl.pallas_call(kernel, out_shape=(jax.ShapeDtypeStruct((NODES, COLS), bf1...  44.2 us
    pallas_call x1, Pallas kernels, shards(): pl.pallas_call(read_back, out_shape=(jax.ShapeDtypeStruct((NODES, COLS),...  2.69 us

profile of v6, /device:TPU:1, one launch (start us, length us, event | category | flops | bytes accessed | tf_op | source)
XLA Modules:
  0.0 48.4 jit_solution(8061886524924399957)
XLA Ops:
  1.3 44.2 %shard_map.239 = (bf16[160,128]{1,0:T(8,128)(2,1)}, bf16[3,768,160]{2,1,0:T(8,128)(2,1)}) custom-call(bf16[3,720,512]{2,1,0:T(8,128)(2,1)} %grid_h.3, s32[720]{0:T(1024)} %fold_h.1, bf16[160,128]{1,0:T(8,128)(2,1)} %mesh_h.1, bf16[5120,512]{1,0:T(8,128)(2,1)} %edge_h.1, bf16[3,3,512,128]{3,2,1,0:T(8,128)(2,1)} %convw_h.1, bf16[1,128]{1,0:T(2,128)(2,1)} %bitcast.11, ...), custom_call_target="tpu_custom_call" | custom-call | tf_op jit(solution)/shard_map/pallas_call | solution.py:452
  45.5 2.7 %shard_map.240 = (bf16[160,128]{1,0:T(8,128)(2,1)}, bf16[3,720,128]{2,1,0:T(8,128)(2,1)}) custom-call(bf16[3,720,512]{2,1,0:T(8,128)(2,1)} %grid_h.3, bf16[3,768,160]{2,1,0:T(8,128)(2,1)} %get-tuple-element.4.rmat_h, bf16[160,128]{1,0:T(8,128)(2,1)} %get-tuple-element.5.node_h), custom_call_target="tpu_custom_call" | custom-call | tf_op jit(solution)/shard_map/pallas_call | solution.py:490
